TPU v7x, 512 devices: a whole 4x4x16 slice. The times are simulated.
512 devices in a mesh: wide: 64 (over z_lo, y, core), narrow: 8 (over z_hi, x).
Axes of the slice: x: 4, y: 4, z: 16 (z_hi: 2, z_lo: 8; z = z_hi * 8 + z_lo), core: 2. Of those that a mesh axis runs over, the one named last changes fastest.
Arguments:
- prior: float32 [384, 32, 384], P('wide', 'narrow'), may hold values from -6 to 6
- coil_maps: bfloat16 [384, 196608], P('wide', 'narrow'), may hold values from -1.5 to 1.5
- kspace: bfloat16 [2, 384, 196608], P(None, None, ('narrow', 'wide')), may hold values from -6 to 6
- band_start: int32 [2, 12288], P(None, ('narrow', 'wide')), may hold values from -12 to 12
- band_frac: float32 [2, 384, 12288], P(None, None, ('narrow', 'wide')), may hold values from 0 to 1
- shot_mask: int32 [2, 6, 32], P(None, None, 'narrow'), may hold values 0 or 1
Outputs:
- solution: float32 [384, 12288], P(None, ('narrow', 'wide'))
- denoised: float32 [384, 32, 384], P('wide', 'narrow')
All inputs are finite; a program needn't handle non-finite values. No bound on the sum of `shot_mask` on one device may be relied on, other than what follows from the above.
Results may differ from a plain program's by a relative error of at most 0.0033.
Values may be sent and summed in bfloat16 or wider, within the bound.
A program may use at most 64 MiB of HBM per device.

v0:
```python
import math

import jax
import jax.numpy as jnp
from jax import lax
from jax.sharding import PartitionSpec as P

BLIPS = 2
SHOTS = 6
TAPS = 8
CG_ITERS = 2
DIFF_STEPS = 3


penalty = 0.5
time_step = 0.18
edge_scale = 1.0
low_offset = -15
band_span = 32
axis_weights = (1.0, 0.5, 1.0)


def padded_2(cells, sides, width):
    for axis, dim in sides:
        count = lax.axis_size(axis)
        ends = count - 1
        head = lax.slice_in_dim(cells, 0, width, axis=dim)
        tail = lax.slice_in_dim(cells, cells.shape[dim] - width, cells.shape[dim], axis=dim)
        cells = jnp.concatenate(
            [
                lax.ppermute(tail, axis, [(i, (i + 1) % count) for i in range(ends)]),
                cells,
                lax.ppermute(head, axis, [((i + 1) % count, i) for i in range(ends)]),
            ],
            axis=dim,
        )
    return cells


def cosine_tables(length):
    freq_pos = jnp.arange(length, dtype=jnp.float32)[:, None]
    cell_pos = jnp.arange(length, dtype=jnp.float32)[None, :]
    entries = jnp.cos(math.pi * (cell_pos + 0.5) * freq_pos / length) * math.sqrt(2.0 / length)
    entries = entries * jnp.where(freq_pos == 0.0, math.sqrt(0.5), 1.0)
    forward = entries.astype(jnp.bfloat16)
    return (forward, jnp.transpose(forward))


def band_coefficients(band_start, band_frac):
    tap_pos = jnp.arange(TAPS, dtype=jnp.float32)[:, None, None, None] - 3.0
    spacing = tap_pos - band_frac[None]
    weights = jnp.sinc(spacing) * jnp.sinc(spacing / 4.0)
    offsets = jnp.arange(band_span, dtype=jnp.int32) + low_offset
    tap_index = offsets[:, None, None] - band_start[None] + 3
    band_coeff = jnp.zeros((band_span,) + band_frac.shape, jnp.float32)
    for tap_no in range(TAPS):
        hit = (tap_index == tap_no)[:, :, None, :]
        band_coeff = band_coeff + jnp.where(hit, weights[tap_no][None], 0.0)
    return band_coeff


def band_apply(band_coeff, values):
    length = values.shape[0]
    padded = jnp.pad(values, ((-low_offset, band_span - 1 + low_offset), (0, 0)))
    summed = jnp.zeros_like(values)
    for offset_no in range(band_span):
        summed = summed + band_coeff[offset_no] * padded[offset_no : offset_no + length]
    return summed


def band_adjoint(band_coeff, values):
    length = values.shape[0]
    summed = jnp.zeros((length + band_span - 1, values.shape[1]), values.dtype)
    for offset_no in range(band_span):
        summed = summed + jnp.pad(
            band_coeff[offset_no] * values, ((offset_no, band_span - 1 - offset_no), (0, 0))
        )
    return summed[-low_offset : -low_offset + length]


def shot_rows(mask_cols, length):
    row_pick = (
        (jnp.arange(length, dtype=jnp.int32) % SHOTS)[:, None]
        == jnp.arange(SHOTS, dtype=jnp.int32)[None, :]
    ).astype(jnp.float32)
    return jnp.einsum("ys,psc->pyc", row_pick, mask_cols)


def coil_return(kept_spec, coil_maps, cosine_back, band_coeff):
    length, col_count, coils_here = coil_maps.shape
    returned = jnp.dot(cosine_back, kept_spec, preferred_element_type=jnp.float32).reshape(
        length, col_count, coils_here
    )
    combined = jnp.sum(returned * coil_maps, axis=2)
    return band_adjoint(band_coeff, combined)


def normal_product(iterate, coil_maps, band_coeff, sampled, cosine_fwd, cosine_back):
    length, col_count, coils_here = coil_maps.shape
    summed = penalty * iterate
    for blip_no in range(BLIPS):
        shifted = band_apply(band_coeff[:, blip_no], iterate)
        coil_images = (coil_maps * shifted[:, :, None]).astype(jnp.bfloat16)
        spectra = jnp.dot(
            cosine_fwd, coil_images.reshape(length, -1), preferred_element_type=jnp.float32
        )
        kept_spec = (
            spectra.reshape(length, col_count, coils_here) * sampled[blip_no][:, :, None]
        ).astype(jnp.bfloat16)
        summed = summed + coil_return(
            kept_spec.reshape(length, -1), coil_maps, cosine_back, band_coeff[:, blip_no]
        )
    return summed


def data_side(kspace, coil_maps, band_coeff, sampled, cosine_back):
    length, col_count, coils_here = coil_maps.shape
    summed = jnp.zeros((length, col_count), jnp.float32)
    for blip_no in range(BLIPS):
        kept_spec = kspace[blip_no].reshape(length, col_count, coils_here) * sampled[blip_no][
            :, :, None
        ].astype(jnp.bfloat16)
        summed = summed + coil_return(
            kept_spec.reshape(length, -1), coil_maps, cosine_back, band_coeff[:, blip_no]
        )
    return summed


def edge_flux(jump_size):
    scaled = jump_size / edge_scale
    return jump_size / (1.0 + scaled * scaled)


def diffuse_once(padded):
    middle = padded[1:-1, 1:-1, 1:-1]
    neighbours = (
        (padded[2:, 1:-1, 1:-1], padded[:-2, 1:-1, 1:-1]),
        (padded[1:-1, 2:, 1:-1], padded[1:-1, :-2, 1:-1]),
        (padded[1:-1, 1:-1, 2:], padded[1:-1, 1:-1, :-2]),
    )
    change = jnp.zeros_like(middle)
    for weight_axis, pair_cells in zip(axis_weights, neighbours):
        change = change + weight_axis * (
            edge_flux(pair_cells[0] - middle) - edge_flux(middle - pair_cells[1])
        )
    return middle + time_step * change


def global_squares(residue):
    return lax.psum(jnp.sum(residue * residue), ("wide", "narrow"))


def per_device(prior, coil_maps, kspace, band_start, band_frac, shot_mask):
    rows_dev, slices_dev, readout = prior.shape
    wide_count = lax.axis_size("wide")
    length = rows_dev * wide_count
    col_count = slices_dev * readout // wide_count
    cosine_fwd, cosine_back = cosine_tables(length)
    prior_cols = lax.all_to_all(
        prior.reshape(rows_dev, slices_dev * readout),
        "wide",
        split_axis=1,
        concat_axis=0,
        tiled=True,
    )
    maps_cols = lax.all_to_all(coil_maps, "wide", split_axis=1, concat_axis=0, tiled=True).reshape(
        length, col_count, -1
    )
    band_coeff = band_coefficients(band_start, band_frac)
    slice_of = (
        lax.axis_index("wide") * col_count + jnp.arange(col_count, dtype=jnp.int32)
    ) // readout
    slice_pick = (slice_of[:, None] == jnp.arange(slices_dev, dtype=jnp.int32)[None, :]).astype(
        jnp.float32
    )
    mask_cols = jnp.einsum("psz,cz->psc", shot_mask.astype(jnp.float32), slice_pick)
    sampled = shot_rows(mask_cols, length)
    rhs_cols = data_side(kspace, maps_cols, band_coeff, sampled, cosine_back) + penalty * prior_cols

    def normal_apply(iterate):
        return normal_product(iterate, maps_cols, band_coeff, sampled, cosine_fwd, cosine_back)

    iterate = prior_cols
    residue = rhs_cols - normal_apply(iterate)
    direction = residue
    norm_now = global_squares(residue)
    for step_index in range(CG_ITERS):
        mapped = normal_apply(direction)
        step_len = norm_now / lax.psum(jnp.sum(direction * mapped), ("wide", "narrow"))
        iterate = iterate + step_len * direction
        if step_index + 1 < CG_ITERS:
            residue = residue - step_len * mapped
            norm_next = global_squares(residue)
            direction = residue + norm_next / norm_now * direction
            norm_now = norm_next
    bricks = lax.all_to_all(iterate, "wide", split_axis=0, concat_axis=1, tiled=True).reshape(
        rows_dev, slices_dev, readout
    )
    for step_index in range(DIFF_STEPS):
        padded = padded_2(bricks, (("wide", 0), ("narrow", 1)), 1)
        bricks = diffuse_once(jnp.pad(padded, ((0, 0), (0, 0), (1, 1))))
    return (iterate, bricks)


def solution(mesh):
    in_specs = (
        P("wide", "narrow", None),
        P("wide", "narrow"),
        P(None, None, ("narrow", "wide")),
        P(None, ("narrow", "wide")),
        P(None, None, ("narrow", "wide")),
        P(None, None, "narrow"),
    )
    out_specs = (P(None, ("narrow", "wide")), P("wide", "narrow", None))
    return jax.shard_map(
        per_device, mesh=mesh, in_specs=in_specs, out_specs=out_specs, check_vma=False
    )
```

profile of v0, /device:TPU:384, one launch (start us, length us, event | category | flops | bytes accessed | tf_op | source)
XLA Modules:
  0.0 567.4 jit_solution(18209022320374475244)
XLA Ops:
  2.6 11.9 %all-to-all-start = ((f32[64,1,144]{2,1,0:T(1,128)}), f32[64,1,144]{2,1,0:T(1,128)S(1)}, u32[]{:S(2)}, u32[]{:S(2)}) async-start(f32[64,1,144]{2,1,0:T(1,128)} %reshape.327), calls=%async_computation | async-start | bytes 131072 | tf_op jit(solution)/shard_map/all_to_all | solution.py:159
  22.0 11.0 %all-to-all-start.1 = ((bf16[6,64,384]{2,0,1:T(8,128)(2,1)}), bf16[6,64,384]{2,0,1:T(8,128)(2,1)}, u32[]{:S(2)}, u32[]{:S(2)}) async-start(bf16[6,64,384]{2,0,1:T(8,128)(2,1)} %bitcast.20), calls=%async_computation.1 | async-start | bytes 786432 | tf_op jit(solution)/shard_map/all_to_all | solution.py:166
  42.3 10.3 %all-to-all-done.1 = bf16[6,64,384]{2,0,1:T(8,128)(2,1)} async-done(((bf16[6,64,384]{2,0,1:T(8,128)(2,1)}), bf16[6,64,384]{2,0,1:T(8,128)(2,1)}, u32[]{:S(2)}, u32[]{:S(2)}) %all-to-all-start.1) | async-done | bytes 294944 | tf_op jit(solution)/shard_map/all_to_all | solution.py:166
  54.6 4.2 reshape.310
  60.0 4.7 copy.77
  67.8 6.1 %fusion.17 = f32[384,24]{0,1:T(8,128)} fusion(f32[384,24,16]{0,1,2:T(8,128)} %copy.77, bf16[24,16,384]{2,1,0:T(8,128)(2,1)S(1)} %bitcast.1178, f32[384,24]{0,1:T(8,128)} %get-tuple-element.287, f32[384]{0:T(512)S(1)} %get-tuple-element.306, f32[384]{0:T(512)S(1)} %get-tuple-element.307), kind=kOutput, calls=%fused_computation.38 | convolution fusion | flops 228252672 | bytes 961536 | tf_op jit(solution)/shard_map/dot_general | solution.py:91
  78.1 6.2 %fusion.16 = f32[384,24]{0,1:T(8,128)} fusion(f32[384,24,16]{0,1,2:T(8,128)} %copy.77, bf16[24,16,384]{2,1,0:T(8,128)(2,1)} %bitcast.1179, f32[384,24]{0,1:T(8,128)} %get-tuple-element.286, f32[384]{0:T(512)S(1)} %get-tuple-element.306, f32[384]{0:T(512)S(1)} %get-tuple-element.307), kind=kOutput, calls=%fused_computation.37 | convolution fusion | flops 228252672 | bytes 961536 | tf_op jit(solution)/shard_map/dot_general | solution.py:91
  100.7 5.5 fusion.19
  108.2 6.3 %fusion.18 = f32[384,24]{0,1:T(8,128)} fusion(f32[384,24,16]{0,1,2:T(8,128)} %copy.77, bf16[24,16,384]{2,1,0:T(8,128)(2,1)S(1)} %bitcast.1182, f32[384,24]{0,1:T(8,128)} %get-tuple-element.286, f32[384]{0:T(512)S(1)} %get-tuple-element.306, f32[384]{0:T(512)S(1)} %get-tuple-element.307), kind=kOutput, calls=%fused_computation.39 | convolution fusion | flops 228252672 | bytes 961536 | tf_op jit(solution)/shard_map/dot_general | solution.py:91
  118.6 102.1 %all-reduce.262 = (f32[]{:T(128)}, f32[]{:T(128)}) all-reduce(f32[]{:T(128)} %get-tuple-element.8, f32[]{:T(128)} %get-tuple-element.7), channel_id=1, replica_groups=mesh['wide'=64,'narrow'=8] {'wide','narrow'}, use_global_device_ids=true, to_apply=%region_5.7 | all-reduce | flops 2 | bytes 16 | tf_op jit(solution)/shard_map/psum | solution.py:150
  222.6 100.3 %psum.30 = f32[]{:T(128)} all-reduce(f32[]{:T(128)} %multiply_reduce_fusion), channel_id=1, replica_groups=mesh['wide'=64,'narrow'=8] {'wide','narrow'}, use_global_device_ids=true, to_apply=%region_11.13 | all-reduce | flops 1 | bytes 8 | tf_op jit(solution)/shard_map/psum | solution.py:150
  330.9 5.6 fusion.21
  338.5 5.8 %fusion.20 = f32[384,24]{0,1:T(8,128)} fusion(f32[384,24,16]{0,1,2:T(8,128)S(1)} %copy-done.11, bf16[24,16,384]{2,1,0:T(8,128)(2,1)S(1)} %bitcast.1177, f32[384,24]{0,1:T(8,128)} %get-tuple-element.286, f32[384]{0:T(512)S(1)} %get-tuple-element.306, f32[384]{0:T(512)S(1)} %get-tuple-element.307), kind=kOutput, calls=%fused_computation.41 | convolution fusion | flops 228252672 | bytes 961536 | tf_op jit(solution)/shard_map/dot_general | solution.py:91
  348.5 99.4 %psum.31 = f32[]{:T(128)} all-reduce(f32[]{:T(128)} %fusion.161), channel_id=1, replica_groups=mesh['wide'=64,'narrow'=8] {'wide','narrow'}, use_global_device_ids=true, to_apply=%region_15.17 | all-reduce | flops 1 | bytes 8 | tf_op jit(solution)/shard_map/psum | solution.py:189
  449.5 18.4 %all_to_all.48 = f32[64,1,144]{2,1,0:T(1,128)S(1)} all-to-all(f32[64,1,144]{2,1,0:T(1,128)S(1)} %reshape.329), channel_id=1, replica_groups=mesh['wide'=64,'narrow'=8] {'wide'}, dimensions={0} | all-to-all | bytes 73728 | tf_op jit(solution)/shard_map/all_to_all | solution.py:196
  471.4 6.9 %collective-permute-start = (f32[1,4,384]{2,1,0:T(4,128)S(1)}, f32[1,4,384]{2,1,0:T(4,128)S(1)}, u32[]{:S(2)}, u32[]{:S(2)}) collective-permute-start(f32[1,4,384]{2,1,0:T(4,128)S(1)} %slice.1475), channel_id=1, source_target_pairs={{8,0},{16,8},{24,16},{32,24},{40,32},{48,40},{56,48},{64,56},{72,6... | collective-permute-start | bytes 18440 | tf_op jit(solution)/shard_map/ppermute | solution.py:33
  479.6 8.7 %collective-permute-start.2 = (f32[8,1,384]{2,1,0:T(1,128)S(1)}, f32[8,1,384]{2,1,0:T(1,128)S(1)}, u32[]{:S(2)}, u32[]{:S(2)}) collective-permute-start(f32[8,1,384]{2,1,0:T(1,128)S(1)} %get-tuple-element.293), channel_id=1, source_target_pairs={{1,0},{2,1},{3,2},{4,3},{5,4},{6,5},{7,6},{9,8},{10,9},{11,10},{12... | collective-permute-start | bytes 36872 | tf_op jit(solution)/shard_map/ppermute | solution.py:33
  490.2 14.6 %collective-permute-done.3 = f32[8,1,384]{2,1,0:T(1,128)S(1)} collective-permute-done((f32[8,1,384]{2,1,0:T(1,128)S(1)}, f32[8,1,384]{2,1,0:T(1,128)S(1)}, u32[]{:S(2)}, u32[]{:S(2)}) %collective-permute-start.3) | collective-permute-done | bytes 12320 | tf_op jit(solution)/shard_map/ppermute | solution.py:31
  505.2 5.4 collective-permute-start.4
  512.5 6.5 %collective-permute-done.5 = f32[1,4,384]{2,1,0:T(4,128)S(1)} collective-permute-done((f32[1,4,384]{2,1,0:T(4,128)S(1)}, f32[1,4,384]{2,1,0:T(4,128)S(1)}, u32[]{:S(2)}, u32[]{:S(2)}) %collective-permute-start.5) | collective-permute-done | bytes 6176 | tf_op jit(solution)/shard_map/ppermute | solution.py:31
  520.9 3.9 collective-permute-start.7
  524.9 12.5 %collective-permute-done.7 = f32[8,1,384]{2,1,0:T(1,128)S(1)} collective-permute-done((f32[8,1,384]{2,1,0:T(1,128)S(1)}, f32[8,1,384]{2,1,0:T(1,128)S(1)}, u32[]{:S(2)}, u32[]{:S(2)}) %collective-permute-start.7) | collective-permute-done | bytes 12320 | tf_op jit(solution)/shard_map/ppermute | solution.py:31
  542.0 5.8 %collective-permute-done.9 = f32[1,4,384]{2,1,0:T(4,128)S(1)} collective-permute-done((f32[1,4,384]{2,1,0:T(4,128)S(1)}, f32[1,4,384]{2,1,0:T(4,128)S(1)}, u32[]{:S(2)}, u32[]{:S(2)}) %collective-permute-start.9) | collective-permute-done | bytes 6176 | tf_op jit(solution)/shard_map/ppermute | solution.py:31
  553.8 12.5 %collective-permute-done.11 = f32[8,1,384]{2,1,0:T(1,128)S(1)} collective-permute-done((f32[8,1,384]{2,1,0:T(1,128)S(1)}, f32[8,1,384]{2,1,0:T(1,128)S(1)}, u32[]{:S(2)}, u32[]{:S(2)}) %collective-permute-start.11) | collective-permute-done | bytes 12320 | tf_op jit(solution)/shard_map/ppermute | solution.py:31
  (352 shorter events, 86.1 us)
Async XLA Ops:
  0.6 16.3 %copy-start.111 = (s32[2,6,4]{1,2,0:T(4,128)S(1)}, s32[2,6,4]{1,2,0:T(4,128)}, u32[]{:S(2)}) copy-start(s32[2,6,4]{1,2,0:T(4,128)} %param.12) | copy-start | bytes 580
  0.6 17.3 %copy-start.9 = (bf16[2,384,384]{2,1,0:T(8,128)(2,1)S(1)}, bf16[2,384,384]{2,1,0:T(8,128)(2,1)}, u32[]{:S(2)}) copy-start(bf16[2,384,384]{2,1,0:T(8,128)(2,1)} %param.9) | copy-start | bytes 1769476
  0.7 17.3 %copy-start.112 = (s32[2,24]{1,0:T(2,128)S(1)}, s32[2,24]{1,0:T(2,128)}, u32[]{:S(2)}) copy-start(s32[2,24]{1,0:T(2,128)} %param.10) | copy-start | bytes 580
  2.6 19.4 %all-to-all-start = ((f32[64,1,144]{2,1,0:T(1,128)}), f32[64,1,144]{2,1,0:T(1,128)S(1)}, u32[]{:S(2)}, u32[]{:S(2)}) async-start(f32[64,1,144]{2,1,0:T(1,128)} %reshape.327), calls=%async_computation | async-start | bytes 131072 | tf_op jit(solution)/shard_map/all_to_all | solution.py:159
  22.0 30.7 %all-to-all-start.1 = ((bf16[6,64,384]{2,0,1:T(8,128)(2,1)}), bf16[6,64,384]{2,0,1:T(8,128)(2,1)}, u32[]{:S(2)}, u32[]{:S(2)}) async-start(bf16[6,64,384]{2,0,1:T(8,128)(2,1)} %bitcast.20), calls=%async_computation.1 | async-start | bytes 786432 | tf_op jit(solution)/shard_map/all_to_all | solution.py:166
  67.8 9.3 %copy-start.3 = (bf16[384,384]{0,1:T(8,128)(2,1)S(1)}, bf16[384,384]{0,1:T(8,128)(2,1)}, u32[]{:S(2)}) copy-start(bf16[384,384]{0,1:T(8,128)(2,1)} %get-tuple-element.274) | copy-start | bytes 884740
  108.2 8.4 %copy-start.70 = (f32[384,24]{0,1:T(8,128)S(1)}, f32[384,24]{0,1:T(8,128)}, u32[]{:S(2)}) copy-start(f32[384,24]{0,1:T(8,128)} %get-tuple-element.108) | copy-start | bytes 110596
  108.2 8.4 %copy-start.71 = (f32[384,24]{0,1:T(8,128)S(1)}, f32[384,24]{0,1:T(8,128)}, u32[]{:S(2)}) copy-start(f32[384,24]{0,1:T(8,128)} %get-tuple-element.115) | copy-start | bytes 110596
  108.2 8.4 %copy-start.72 = (f32[384,24]{0,1:T(8,128)S(1)}, f32[384,24]{0,1:T(8,128)}, u32[]{:S(2)}) copy-start(f32[384,24]{0,1:T(8,128)} %get-tuple-element.116) | copy-start | bytes 110596
  344.5 104.6 %copy-start.2 = (f32[384,24]{0,1:T(8,128)S(1)}, f32[384,24]{0,1:T(8,128)}, u32[]{:S(2)}) copy-start(f32[384,24]{0,1:T(8,128)} %copy-done) | copy-start | bytes 110596
  344.5 104.6 %copy-start.6 = (f32[384,24]{0,1:T(8,128)S(1)}, f32[384,24]{0,1:T(8,128)}, u32[]{:S(2)}) copy-start(f32[384,24]{0,1:T(8,128)} %copy-done.4) | copy-start | bytes 110596
  449.1 118.0 %copy-start.110 = (f32[384,24]{0,1:T(8,128)}, f32[384,24]{0,1:T(8,128)S(1)}, u32[]{:S(2)}) copy-start(f32[384,24]{0,1:T(8,128)S(1)} %multiply_add_fusion.5) | copy-start | bytes 110596
  469.1 9.2 %collective-permute-start.1 = (f32[1,4,384]{2,1,0:T(4,128)S(1)}, f32[1,4,384]{2,1,0:T(4,128)S(1)}, u32[]{:S(2)}, u32[]{:S(2)}) collective-permute-start(f32[1,4,384]{2,1,0:T(4,128)S(1)} %slice.1478), channel_id=1, source_target_pairs={{0,8},{8,16},{16,24},{24,32},{32,40},{40,48},{48,56},{56,64},{64,7... | collective-permute-start | bytes 18440 | tf_op jit(solution)/shard_map/ppermute | solution.py:31
  471.4 8.2 %collective-permute-start = (f32[1,4,384]{2,1,0:T(4,128)S(1)}, f32[1,4,384]{2,1,0:T(4,128)S(1)}, u32[]{:S(2)}, u32[]{:S(2)}) collective-permute-start(f32[1,4,384]{2,1,0:T(4,128)S(1)} %slice.1475), channel_id=1, source_target_pairs={{8,0},{16,8},{24,16},{32,24},{40,32},{48,40},{56,48},{64,56},{72,6... | collective-permute-start | bytes 18440 | tf_op jit(solution)/shard_map/ppermute | solution.py:33
  479.6 10.6 %collective-permute-start.2 = (f32[8,1,384]{2,1,0:T(1,128)S(1)}, f32[8,1,384]{2,1,0:T(1,128)S(1)}, u32[]{:S(2)}, u32[]{:S(2)}) collective-permute-start(f32[8,1,384]{2,1,0:T(1,128)S(1)} %get-tuple-element.293), channel_id=1, source_target_pairs={{1,0},{2,1},{3,2},{4,3},{5,4},{6,5},{7,6},{9,8},{10,9},{11,10},{12... | collective-permute-start | bytes 36872 | tf_op jit(solution)/shard_map/ppermute | solution.py:33
  488.3 16.5 %collective-permute-start.3 = (f32[8,1,384]{2,1,0:T(1,128)S(1)}, f32[8,1,384]{2,1,0:T(1,128)S(1)}, u32[]{:S(2)}, u32[]{:S(2)}) collective-permute-start(f32[8,1,384]{2,1,0:T(1,128)S(1)} %get-tuple-element.292), channel_id=1, source_target_pairs={{0,1},{1,2},{2,3},{3,4},{4,5},{5,6},{6,7},{8,9},{9,10},{10,11},{11... | collective-permute-start | bytes 36872 | tf_op jit(solution)/shard_map/ppermute | solution.py:31
  505.2 7.3 %collective-permute-start.4 = (f32[1,4,384]{2,1,0:T(4,128)S(1)}, f32[1,4,384]{2,1,0:T(4,128)S(1)}, u32[]{:S(2)}, u32[]{:S(2)}) collective-permute-start(f32[1,4,384]{2,1,0:T(4,128)S(1)} %get-tuple-element.297), channel_id=1, source_target_pairs={{8,0},{16,8},{24,16},{32,24},{40,32},{48,40},{56,48},{64,56},{72,6... | collective-permute-start | bytes 18440 | tf_op jit(solution)/shard_map/ppermute | solution.py:33
  510.6 8.4 %collective-permute-start.5 = (f32[1,4,384]{2,1,0:T(4,128)S(1)}, f32[1,4,384]{2,1,0:T(4,128)S(1)}, u32[]{:S(2)}, u32[]{:S(2)}) collective-permute-start(f32[1,4,384]{2,1,0:T(4,128)S(1)} %get-tuple-element.296), channel_id=1, source_target_pairs={{0,8},{8,16},{16,24},{24,32},{32,40},{40,48},{48,56},{56,64},{64,7... | collective-permute-start | bytes 18440 | tf_op jit(solution)/shard_map/ppermute | solution.py:31
  519.0 5.9 %collective-permute-start.6 = (f32[8,1,384]{2,1,0:T(1,128)S(1)}, f32[8,1,384]{2,1,0:T(1,128)S(1)}, u32[]{:S(2)}, u32[]{:S(2)}) collective-permute-start(f32[8,1,384]{2,1,0:T(1,128)S(1)} %get-tuple-element.291), channel_id=1, source_target_pairs={{1,0},{2,1},{3,2},{4,3},{5,4},{6,5},{7,6},{9,8},{10,9},{11,10},{12... | collective-permute-start | bytes 36872 | tf_op jit(solution)/shard_map/ppermute | solution.py:33
  520.9 16.4 %collective-permute-start.7 = (f32[8,1,384]{2,1,0:T(1,128)S(1)}, f32[8,1,384]{2,1,0:T(1,128)S(1)}, u32[]{:S(2)}, u32[]{:S(2)}) collective-permute-start(f32[8,1,384]{2,1,0:T(1,128)S(1)} %get-tuple-element.290), channel_id=1, source_target_pairs={{0,1},{1,2},{2,3},{3,4},{4,5},{5,6},{6,7},{8,9},{9,10},{10,11},{11... | collective-permute-start | bytes 36872 | tf_op jit(solution)/shard_map/ppermute | solution.py:31
  537.7 4.3 collective-permute-start.8
  539.6 8.3 %collective-permute-start.9 = (f32[1,4,384]{2,1,0:T(4,128)S(1)}, f32[1,4,384]{2,1,0:T(4,128)S(1)}, u32[]{:S(2)}, u32[]{:S(2)}) collective-permute-start(f32[1,4,384]{2,1,0:T(4,128)S(1)} %get-tuple-element.294), channel_id=1, source_target_pairs={{0,8},{8,16},{16,24},{24,32},{32,40},{40,48},{48,56},{56,64},{64,7... | collective-permute-start | bytes 18440 | tf_op jit(solution)/shard_map/ppermute | solution.py:31
  547.9 5.9 %collective-permute-start.10 = (f32[8,1,384]{2,1,0:T(1,128)S(1)}, f32[8,1,384]{2,1,0:T(1,128)S(1)}, u32[]{:S(2)}, u32[]{:S(2)}) collective-permute-start(f32[8,1,384]{2,1,0:T(1,128)S(1)} %get-tuple-element.289), channel_id=1, source_target_pairs={{1,0},{2,1},{3,2},{4,3},{5,4},{6,5},{7,6},{9,8},{10,9},{11,10},{12... | collective-permute-start | bytes 36872 | tf_op jit(solution)/shard_map/ppermute | solution.py:33
  549.8 16.4 %collective-permute-start.11 = (f32[8,1,384]{2,1,0:T(1,128)S(1)}, f32[8,1,384]{2,1,0:T(1,128)S(1)}, u32[]{:S(2)}, u32[]{:S(2)}) collective-permute-start(f32[8,1,384]{2,1,0:T(1,128)S(1)} %get-tuple-element.288), channel_id=1, source_target_pairs={{0,1},{1,2},{2,3},{3,4},{4,5},{5,6},{6,7},{8,9},{9,10},{10,11},{11... | collective-permute-start | bytes 36872 | tf_op jit(solution)/shard_map/ppermute | solution.py:31
  (103 other events, 323.9 us)
where the time goes:
time: 576 us; the launch traced here: 567 us
  blocking collectives  320 us (56%)
  starting transfers between devices  65.7 us (11%)
  waiting for transfers between devices  65.7 us (11%)
  matrix products  40.9 us (7%)
  other arithmetic  39.8 us (7%)
  local copies, waits for them, and re-layouts  28.2 us (5%)
  between operations  6.89 us (1%)
    psum x2, blocking collectives, global_squares(): return lax.psum(jnp.sum(residue * residue), ('wide', 'narrow'))  202 us
    psum x1, blocking collectives, per_device(): lax.psum(jnp.sum(direction * mapped), ('wide', 'narrow'))  99.4 us
    ppermute x6, waiting for transfers between devices, padded_2(): lax.ppermute(tail, axis, [(i, (i + 1) % count) for i in range(ends)])  51.9 us
    dot_general x8, matrix products, coil_return(): jnp.dot(cosine_back, kept_spec, preferred_element_type=jnp.float32)  40.6 us
    ppermute x6, starting transfers between devices, padded_2(): lax.ppermute(head, axis, [((i + 1) % count, i) for i in range(ends)])  26.7 us
    all_to_all x1, blocking collectives, per_device(): lax.all_to_all(iterate, 'wide', split_axis=0, concat_axis=1, tiled=True)  18.4 us
    ppermute x6, starting transfers between devices, padded_2(): lax.ppermute(tail, axis, [(i, (i + 1) % count) for i in range(ends)])  16.1 us
    mul x16, other arithmetic, band_adjoint(): band_coeff[offset_no] * values  12 us
  transfers between devices with their start and end apart: 14, of which 8 were waited for; matrix products, arithmetic and copies ran while one was open for 2% of the time, Pallas kernels for 0%

commit v1 on v0

v1 whole, which is shorter than its diff:
```python
import functools
import math

import jax
import jax.numpy as jnp
import numpy as np
from jax import lax
from jax.experimental import pallas as pl
from jax.experimental.pallas import tpu as pltpu
from jax.sharding import PartitionSpec as P

SHOTS = 6
TAPS = 8
DIFF_STEPS = 3
COILS = 16
WIDE = 64
NARROW = 8
LINES = 384
COLS = 24
ROWS = 6
SLICES = 4
READOUT = 384
SPAN = 512
PIECES = 3
BAND_BITS = 5

penalty = 0.5
time_step = 0.18
axis_weights = (1.0, 0.5, 1.0)

F32 = jnp.float32
BF16 = jnp.bfloat16
MESH = pl.DeviceIdType.MESH


def cosine_table():
    freq = np.arange(LINES, dtype=np.float32)[:, None]
    cell = np.arange(LINES, dtype=np.float32)[None, :]
    angle = np.float32(math.pi) * (cell + np.float32(0.5)) * freq / np.float32(LINES)
    entries = np.cos(angle).astype(np.float32) * np.float32(math.sqrt(2.0 / LINES))
    entries = entries * np.where(freq == 0.0, np.float32(math.sqrt(0.5)), np.float32(1.0))
    return entries.astype(np.float32)


def place_tables():
    place = np.zeros((WIDE * 8, LINES + 128), np.float32)
    for w in range(WIDE):
        for i in range(ROWS):
            place[8 * w + i, ROWS * w + i] = 1.0
        for g in range(2):
            place[8 * w + 6 + g, LINES + g * 64 + w] = 1.0
    order = np.zeros((3 * 128, LINES), np.float32)
    for t in range(3):
        for g in range(2):
            for w in range(WIDE):
                order[t * 128 + g * 64 + w, ROWS * w + 3 * g + t] = 1.0
    return place, order


def lane_iota(rows, lanes):
    return lax.broadcasted_iota(jnp.int32, (rows, lanes), 1)


def gather_body(prior_ref, maps_ref, out_ref, send_buf, own_sem, send_sem, recv_sem):
    me = lax.axis_index("wide")
    barrier = pltpu.get_barrier_semaphore()

    @pl.loop(1, WIDE)
    def _(k):
        pl.semaphore_signal(barrier, inc=1, device_id={"wide": lax.rem(me + k, WIDE)}, device_id_type=MESH)

    lane = lane_iota(8, 128)
    stacked = [jnp.concatenate([prior_ref[t], prior_ref[3 + t]], axis=0) for t in range(3)]
    for q in range(16):
        packed = jnp.zeros((8, 128), F32)
        for t in range(3):
            turned = pltpu.roll(stacked[t], (24 * t - 24 * q) % READOUT, 1)[:, :128]
            packed = jnp.where((lane >= 24 * t) & (lane < 24 * t + 24), turned, packed)
        high = packed.astype(BF16).astype(F32)
        rest = packed - high
        middle = rest.astype(BF16).astype(F32)
        low = rest - middle
        packed = jnp.concatenate([high, middle, low], axis=1)
        for s in range(SLICES):
            d = 16 * s + q
            block = maps_ref[:, d * 384 : (d + 1) * 384].astype(F32)
            message = jnp.concatenate([block, packed[s : s + 1], packed[4 + s : 5 + s]], axis=0)
            send_buf[d] = message.astype(BF16)

    pl.semaphore_wait(barrier, WIDE - 1)

    @pl.loop(1, WIDE)
    def _(k):
        to = lax.rem(me + k, WIDE)
        pltpu.make_async_remote_copy(
            src_ref=send_buf.at[to],
            dst_ref=out_ref.at[me],
            send_sem=send_sem,
            recv_sem=recv_sem,
            device_id={"wide": to},
            device_id_type=MESH,
        ).start()

    own = pltpu.make_async_copy(send_buf.at[me], out_ref.at[me], own_sem)
    own.start()
    own.wait()
    others = pl.ds(0, WIDE - 1)
    pltpu.make_async_copy(send_buf.at[others], send_buf.at[others], send_sem).wait()
    pltpu.make_async_copy(out_ref.at[others], out_ref.at[others], recv_sem).wait()


def gather_columns(prior, coil_maps):
    vmem = pl.BlockSpec(memory_space=pltpu.VMEM)
    return pl.pallas_call(
        gather_body,
        out_shape=jax.ShapeDtypeStruct((WIDE, 8, LINES), BF16),
        in_specs=[vmem, vmem],
        out_specs=vmem,
        scratch_shapes=[
            pltpu.VMEM((WIDE, 8, LINES), BF16),
            pltpu.SemaphoreType.DMA,
            pltpu.SemaphoreType.DMA,
            pltpu.SemaphoreType.DMA,
        ],
        compiler_params=pltpu.CompilerParams(collective_id=0, has_side_effects=True, vmem_limit_bytes=24 << 20),
        name="gather_columns",
    )(prior, coil_maps)


def poly_sin(x):
    x2 = x * x
    return x * (1.0 + x2 * (-1.0 / 6 + x2 * (1.0 / 120 + x2 * (-1.0 / 5040 + x2 * (1.0 / 362880)))))


def poly_cos(x):
    x2 = x * x
    return 1.0 + x2 * (-0.5 + x2 * (1.0 / 24 + x2 * (-1.0 / 720 + x2 * (1.0 / 40320 - x2 * (1.0 / 3628800)))))


def tap_weights(frac):
    near = jnp.minimum(frac, 1.0 - frac) * (math.pi / 2)
    full = 2.0 * poly_sin(near) * poly_cos(near)
    phi = frac * (math.pi / 4)
    sin_a, cos_a = poly_sin(phi), poly_cos(phi)
    rest = (1.0 - frac) * (math.pi / 4)
    sin_b, cos_b = poly_sin(rest), poly_cos(rest)
    quarter = {-3: -sin_b, -2: -cos_a, -1: -cos_b, 0: -sin_a, 1: sin_b, 2: cos_a, 3: cos_b, 4: sin_a}
    weights = []
    for k in range(TAPS):
        n = k - 3
        t = n - frac
        sign = 1.0 if n % 2 else -1.0
        if n in (0, 1):
            small = jnp.abs(t) < 1e-5
            inverse = 1.0 / jnp.where(small, 1.0, t)
            product = (full * inverse) * (quarter[n] * inverse) * (sign * 4.0 / math.pi**2)
            weights.append(jnp.where(small, 1.0, product))
        else:
            inverse = 1.0 / t
            weights.append((full * inverse) * (quarter[n] * inverse) * (sign * 4.0 / math.pi**2))
    return weights


def wide_lines(values):
    return jnp.concatenate([values, jnp.zeros((values.shape[0], SPAN - LINES), F32)], axis=1)


def left(values, count):
    return pltpu.roll(values, (SPAN - count) % SPAN, 1) if count % SPAN else values


def split3(values):
    high = values.astype(BF16)
    rest = values - high.astype(F32)
    middle = rest.astype(BF16)
    low = (rest - middle.astype(F32)).astype(BF16)
    return high, middle, low


def dot(a, b):
    return jnp.dot(a, b, preferred_element_type=F32)


def dot_first(a, b):
    return lax.dot_general(a, b, (((0,), (0,)), ((), ())), preferred_element_type=F32)


def solve_body(
    got_ref, kspace_ref, start_ref, frac_ref, mask_ref, table_ref, turned_ref, place_ref, order_ref,
    fields_ref, prior_ref, sums_ref, maps3_ref, weight_ref, kept_ref,
):
    my_slice = lax.axis_index("wide") // 16
    both = 2 * COLS

    starts = []
    diagonal = lax.broadcasted_iota(jnp.int32, (COLS, COLS), 0) == lax.broadcasted_iota(jnp.int32, (COLS, COLS), 1)
    for p in range(2):
        row = jnp.broadcast_to(start_ref[p : p + 1, :].astype(F32), (COLS, COLS))
        starts.append(jnp.sum(jnp.where(diagonal, row, 0.0), axis=1, keepdims=True))
    ahead = jnp.concatenate(starts, axis=0).astype(jnp.int32) + 12
    bits = [jnp.broadcast_to((ahead >> bit) & 1, (both, SPAN)) == 1 for bit in range(BAND_BITS)]

    frac = jnp.concatenate([frac_ref[0], frac_ref[1]], axis=0)
    for k, weight in enumerate(tap_weights(frac)):
        weight_ref[k] = weight

    lane = lane_iota(1, LINES)
    shot = lax.rem(lane, SHOTS)
    masks = []
    for p in range(2):
        row = jnp.zeros((1, LINES), F32)
        for h in range(SHOTS):
            row = jnp.where(shot == h, mask_ref[p, my_slice, h].astype(F32), row)
        masks.append(row)
    turned = turned_ref[...]
    forward = [(turned.astype(F32) * masks[p]).astype(BF16) for p in range(2)]

    got = got_ref[...].reshape(WIDE * 8, LINES)
    laid = dot_first(got, place_ref[...])
    maps3_ref[...] = laid[:, :LINES].reshape(COLS, COILS, LINES)
    pieces = []
    for m in range(PIECES):
        parts = [laid[m * 128 + 24 * t : m * 128 + 24 * t + 24, LINES:] for t in range(3)]
        pieces.append(jnp.concatenate(parts, axis=1))
    ordered = dot(jnp.concatenate(pieces, axis=0).astype(BF16), order_ref[...])
    prior = ordered[:COLS] + ordered[COLS : 2 * COLS] + ordered[2 * COLS :]
    prior_ref[...] = prior

    def band_apply(field):
        value = wide_lines(jnp.concatenate([field, field], axis=0))
        value = left(value, -15)
        for bit in range(BAND_BITS):
            value = jnp.where(bits[bit], left(value, 1 << bit), value)
        total = jnp.zeros((both, LINES), F32)
        for k in range(TAPS):
            total = total + weight_ref[k] * left(value, k)[:, :LINES]
        return total

    def band_adjoint(values):
        total = jnp.zeros((both, SPAN), F32)
        for k in range(TAPS):
            total = total + left(wide_lines(weight_ref[k] * values), -k)
        for bit in range(BAND_BITS):
            total = jnp.where(bits[bit], left(total, -(1 << bit)), total)
        total = left(total, 15)
        return (total[:COLS] + total[COLS:])[:, :LINES]

    def through(field):
        moved = band_apply(field)
        back = []
        for p in range(2):
            image = maps3_ref[...] * moved[p * COLS : (p + 1) * COLS][:, None, :]
            image = image.reshape(COLS * COILS, LINES).astype(BF16)
            kept = dot(image, forward[p]).astype(BF16)
            back.append(dot(kept, table_ref[...]))
        return back

    def combine(back):
        return jnp.sum(back.reshape(COLS, COILS, LINES) * maps3_ref[...], axis=1)

    for p in range(2):
        masked = kspace_ref[p]
        kept_ref[p] = lax.dot_general(
            masked, forward[p], (((0,), (1,)), ((), ())), preferred_element_type=F32
        )
    back = through(prior)
    residue = band_adjoint(jnp.concatenate([combine(kept_ref[p] - back[p]) for p in range(2)], axis=0))
    back = through(residue)
    first = band_adjoint(jnp.concatenate([combine(back[p]) for p in range(2)], axis=0))
    back = through(first)
    second = band_adjoint(jnp.concatenate([combine(back[p]) for p in range(2)], axis=0))
    fields_ref[...] = jnp.concatenate([residue, first], axis=0)

    def total(values):
        folded = jnp.sum(values.reshape(3, 8, LINES), axis=0)
        folded = folded[:, :128] + folded[:, 128:256] + folded[:, 256:]
        return jnp.sum(folded, axis=0, keepdims=True)

    sums = [total(residue * residue), total(residue * first), total(first * first), total(first * second)]
    sums_ref[...] = jnp.concatenate(sums + [jnp.zeros((4, 128), F32)], axis=0)


def solve_columns(got, kspace, band_start, frac, mask):
    vmem = pl.BlockSpec(memory_space=pltpu.VMEM)
    table = cosine_table()
    place, order = place_tables()
    return pl.pallas_call(
        solve_body,
        out_shape=(
            jax.ShapeDtypeStruct((2 * COLS, LINES), F32),
            jax.ShapeDtypeStruct((COLS, LINES), F32),
            jax.ShapeDtypeStruct((8, 128), F32),
        ),
        in_specs=[vmem] * 4 + [pl.BlockSpec(memory_space=pltpu.SMEM)] + [vmem] * 4,
        out_specs=(vmem, vmem, vmem),
        scratch_shapes=[
            pltpu.VMEM((COLS, COILS, LINES), F32),
            pltpu.VMEM((TAPS, 2 * COLS, LINES), F32),
            pltpu.VMEM((2, COLS * COILS, LINES), F32),
        ],
        compiler_params=pltpu.CompilerParams(vmem_limit_bytes=48 << 20),
        name="solve_columns",
    )(
        got, kspace, band_start, frac, mask,
        jnp.asarray(table, BF16), jnp.asarray(table.T, BF16), jnp.asarray(place, BF16), jnp.asarray(order, BF16),
    )


def step_scalars(rr, ra, aa, ab):
    alpha = rr / (penalty * rr + ra)
    rho = ra / rr
    qq = jnp.maximum(aa - rho * ra, 0.0)
    qaq = ab - 2.0 * rho * aa + rho * rho * ra
    next_rr = alpha * alpha * qq
    beta = next_rr / rr
    direction_sq = next_rr + beta * beta * rr
    direction_a = alpha * alpha * qaq - 2.0 * beta * alpha * qq + beta * beta * ra
    image = jnp.maximum(penalty * direction_sq + direction_a, penalty * direction_sq)
    second = jnp.where(image > 0.0, next_rr / jnp.where(image > 0.0, image, 1.0), 0.0)
    return alpha + second * (alpha * rho + beta), -second * alpha


def padded_2(cells, sides, width):
    for axis, dim in sides:
        count = lax.axis_size(axis)
        ends = count - 1
        head = lax.slice_in_dim(cells, 0, width, axis=dim)
        tail = lax.slice_in_dim(cells, cells.shape[dim] - width, cells.shape[dim], axis=dim)
        cells = jnp.concatenate(
            [
                lax.ppermute(tail, axis, [(i, (i + 1) % count) for i in range(ends)]),
                cells,
                lax.ppermute(head, axis, [((i + 1) % count, i) for i in range(ends)]),
            ],
            axis=dim,
        )
    return cells


def edge_flux(jump):
    return jump / (1.0 + jump * jump)


def diffuse_once(padded):
    middle = padded[1:-1, 1:-1, 1:-1]
    neighbours = (
        (padded[2:, 1:-1, 1:-1], padded[:-2, 1:-1, 1:-1]),
        (padded[1:-1, 2:, 1:-1], padded[1:-1, :-2, 1:-1]),
        (padded[1:-1, 1:-1, 2:], padded[1:-1, 1:-1, :-2]),
    )
    change = jnp.zeros_like(middle)
    for weight_axis, pair_cells in zip(axis_weights, neighbours):
        change = change + weight_axis * (edge_flux(pair_cells[0] - middle) - edge_flux(middle - pair_cells[1]))
    return middle + time_step * change


def per_device(prior, coil_maps, kspace, band_start, band_frac, shot_mask):
    got = gather_columns(prior, coil_maps)
    fields, prior_cols, sums = solve_columns(
        got, kspace, band_start, jnp.transpose(band_frac, (0, 2, 1)), jnp.transpose(shot_mask, (0, 2, 1))
    )
    sums = lax.psum(jnp.sum(sums, axis=1), ("wide", "narrow"))
    c0, c1 = step_scalars(sums[0], sums[1], sums[2], sums[3])
    iterate = jnp.transpose(prior_cols + c0 * fields[:COLS] + c1 * fields[COLS:])
    bricks = lax.all_to_all(iterate, "wide", split_axis=0, concat_axis=1, tiled=True).reshape(ROWS, SLICES, READOUT)
    for _ in range(DIFF_STEPS):
        padded = padded_2(bricks, (("wide", 0), ("narrow", 1)), 1)
        bricks = diffuse_once(jnp.pad(padded, ((0, 0), (0, 0), (1, 1))))
    return iterate, bricks


def solution(mesh):
    in_specs = (
        P("wide", "narrow", None),
        P("wide", "narrow"),
        P(None, None, ("narrow", "wide")),
        P(None, ("narrow", "wide")),
        P(None, None, ("narrow", "wide")),
        P(None, None, "narrow"),
    )
    out_specs = (P(None, ("narrow", "wide")), P("wide", "narrow", None))
    return jax.shard_map(per_device, mesh=mesh, in_specs=in_specs, out_specs=out_specs, check_vma=False)
```

time: 576 us -> 270 us (0.47); the launches traced: 567 us -> 269 us
  blocking collectives: 320 us -> 120 us
  matrix products: 40.9 us -> 0 us
  other arithmetic: 39.8 us -> 2.54 us
  Pallas kernels: 0 us -> 34.5 us
  starting transfers between devices: 65.7 us -> 41.3 us
  local copies, waits for them, and re-layouts: 28.2 us -> 9.05 us
  waiting for transfers between devices: 65.7 us -> 53.2 us
    psum x3 -> x1, blocking collectives: 302 us -> 104 us  [per_device(): sums = lax.psum(jnp.sum(sums, axis=1), ('wide', 'narrow'))]
    dot_general x9 -> x0, matrix products: 40.9 us -> none  [the longest x8 40.6 us: coil_return(): jnp.dot(cosine_back, kept_spec, preferred_element_type=jnp.float32)]
    pallas_call x0 -> x2, Pallas kernels: none -> 34.5 us  [the longest x1 26.3 us: gather_columns(): pl.pallas_call(gather_body, out_shape=jax.ShapeDtypeStruct((WIDE, 8, LINE...]
    all_to_all x2 -> x0, starting transfers between devices: 22.9 us -> none  [the longest x1 11.9 us: per_device(): lax.all_to_all(prior.reshape(rows_dev, slices_dev * readout), 'wide', spl...]
    mul x19 -> x0, other arithmetic: 15.3 us -> none  [the longest x16 12 us: band_adjoint(): band_coeff[offset_no] * values]
    all_to_all x2 -> x0, waiting for transfers between devices: 12.6 us -> none  [the longest x1 10.3 us: per_device(): lax.all_to_all(coil_maps, 'wide', split_axis=1, concat_axis=0, tiled=True)]
    add x18 -> x0, other arithmetic: 11.6 us -> none  [the longest x6 6.41 us: band_apply(): summed + band_coeff[offset_no] * padded[offset_no:offset_no + length]]
    convert_element_type x4 -> x0, local copies, waits for them, and re-layouts: 10.1 us -> none  [the longest x3 10.1 us: coil_return(): combined = jnp.sum(returned * coil_maps, axis=2)]
  transfers between devices with their start and end apart: 14 -> 12, of which waited for: 8 -> 6; matrix products, arithmetic and copies ran while one was open for 2% -> 0% of each run, Pallas kernels for 0% -> 0%
where the time goes in v1:
time: 270 us; the launch traced here: 269 us
  blocking collectives  120 us (44%)
  waiting for transfers between devices  53.2 us (20%)
  starting transfers between devices  41.3 us (15%)
  Pallas kernels  34.5 us (13%)
  local copies, waits for them, and re-layouts  9.05 us (3%)
  between operations  8.98 us (3%)
    psum x1, blocking collectives, per_device(): sums = lax.psum(jnp.sum(sums, axis=1), ('wide', 'narrow'))  104 us
    ppermute x6, waiting for transfers between devices, padded_2(): lax.ppermute(tail, axis, [(i, (i + 1) % count) for i in range(ends)])  51.9 us
    pallas_call x1, Pallas kernels, gather_columns(): pl.pallas_call(gather_body, out_shape=jax.ShapeDtypeStruct((WIDE, 8, LINE...  26.3 us
    ppermute x6, starting transfers between devices, padded_2(): lax.ppermute(head, axis, [((i + 1) % count, i) for i in range(ends)])  25.2 us
    ppermute x6, starting transfers between devices, padded_2(): lax.ppermute(tail, axis, [(i, (i + 1) % count) for i in range(ends)])  16.1 us
    all_to_all x1, blocking collectives, per_device(): lax.all_to_all(iterate, 'wide', split_axis=0, concat_axis=1, tiled=True)  15.9 us
    pallas_call x1, Pallas kernels, solve_columns(): pl.pallas_call(solve_body, out_shape=(jax.ShapeDtypeStruct((2 * COLS, LIN...  8.21 us
    unnamed x26, local copies, waits for them, and re-layouts  7.2 us
  transfers between devices with their start and end apart: 12, of which 6 were waited for; matrix products, arithmetic and copies ran while one was open for 0% of the time, Pallas kernels for 0%

profile of v1, /device:TPU:384, one launch (start us, length us, event | category | flops | bytes accessed | tf_op | source)
XLA Modules:
  0.0 269.0 jit_solution(14453597471567204265)
XLA Ops:
  0.7 1.0 copy-done.2
  2.5 26.3 %gather_columns.1.got_ref = bf16[64,8,384]{2,1,0:T(8,128)(2,1)S(1)} custom-call(f32[6,4,384]{2,1,0:T(4,128)S(1)} %copy-done.7, bf16[6,24576]{1,0:T(8,128)(2,1)S(1)} %copy-done.2), custom_call_target="tpu_custom_call" | custom-call | tf_op jit(solution)/shard_map/gather_columns/pallas_call | solution.py:114
  29.4 1.0 copy-done.1
  33.4 8.2 %solve_columns.1 = (f32[48,384]{1,0:T(8,128)S(1)}, f32[24,384]{1,0:T(8,128)S(1)}, f32[8,128]{1,0:T(8,128)S(1)}) custom-call(bf16[64,8,384]{2,1,0:T(8,128)(2,1)S(1)} %gather_columns.1.got_ref, bf16[2,384,384]{2,1,0:T(8,128)(2,1)S(1)} %copy-done, s32[2,24]{1,0:T(2,128)S(1)} %copy-done.9, f32[2,24,384]{2,1,0:T(8,128)S(1)} %bitcast.9, s32[2,4,6]{2,1,0:T(4,128)S(1)} %bitcast.10, ...), custom_call_target="tpu_custom_call" | custom-call | tf_op jit(solution)/shard_map/solve_columns/pallas_call | solution.py:287
  41.7 103.6 %psum.7 = f32[8]{0:T(128)S(1)} all-reduce(f32[8]{0:T(128)S(1)} %reduce_sum.9), channel_id=1, replica_groups=mesh['wide'=64,'narrow'=8] {'wide','narrow'}, use_global_device_ids=true, to_apply=%region_1.0 | all-reduce | flops 8 | bytes 64 | tf_op jit(solution)/shard_map/psum | solution.py:362
  154.7 15.9 %all_to_all.16 = f32[64,1,144]{2,1,0:T(1,128)S(1)} all-to-all(f32[64,1,144]{2,1,0:T(1,128)S(1)} %reshape.26), channel_id=1, replica_groups=mesh['wide'=64,'narrow'=8] {'wide'}, dimensions={0} | all-to-all | bytes 73728 | tf_op jit(solution)/shard_map/all_to_all | solution.py:365
  172.4 2.0 collective-permute-start.1
  174.7 6.9 %collective-permute-start = (f32[1,4,384]{2,1,0:T(4,128)S(1)}, f32[1,4,384]{2,1,0:T(4,128)S(1)}, u32[]{:S(2)}, u32[]{:S(2)}) collective-permute-start(f32[1,4,384]{2,1,0:T(4,128)S(1)} %slice.160), channel_id=1, source_target_pairs={{8,0},{16,8},{24,16},{32,24},{40,32},{48,40},{56,48},{64,56},{72,6... | collective-permute-start | bytes 18440 | tf_op jit(solution)/shard_map/ppermute | solution.py:333
  181.6 1.3 collective-permute-done
  182.9 7.2 %collective-permute-start.2 = (f32[8,1,384]{2,1,0:T(1,128)S(1)}, f32[8,1,384]{2,1,0:T(1,128)S(1)}, u32[]{:S(2)}, u32[]{:S(2)}) collective-permute-start(f32[8,1,384]{2,1,0:T(1,128)S(1)} %get-tuple-element.15), channel_id=1, source_target_pairs={{1,0},{2,1},{3,2},{4,3},{5,4},{6,5},{7,6},{9,8},{10,9},{11,10},{12... | collective-permute-start | bytes 36872 | tf_op jit(solution)/shard_map/ppermute | solution.py:333
  190.1 1.9 collective-permute-start.3
  192.1 14.6 %collective-permute-done.3 = f32[8,1,384]{2,1,0:T(1,128)S(1)} collective-permute-done((f32[8,1,384]{2,1,0:T(1,128)S(1)}, f32[8,1,384]{2,1,0:T(1,128)S(1)}, u32[]{:S(2)}, u32[]{:S(2)}) %collective-permute-start.3) | collective-permute-done | bytes 12320 | tf_op jit(solution)/shard_map/ppermute | solution.py:331
  207.0 5.4 %collective-permute-start.4 = (f32[1,4,384]{2,1,0:T(4,128)S(1)}, f32[1,4,384]{2,1,0:T(4,128)S(1)}, u32[]{:S(2)}, u32[]{:S(2)}) collective-permute-start(f32[1,4,384]{2,1,0:T(4,128)S(1)} %get-tuple-element.19), channel_id=1, source_target_pairs={{8,0},{16,8},{24,16},{32,24},{40,32},{48,40},{56,48},{64,56},{72,6... | collective-permute-start | bytes 18440 | tf_op jit(solution)/shard_map/ppermute | solution.py:333
  212.4 1.9 collective-permute-start.5
  214.4 6.5 %collective-permute-done.5 = f32[1,4,384]{2,1,0:T(4,128)S(1)} collective-permute-done((f32[1,4,384]{2,1,0:T(4,128)S(1)}, f32[1,4,384]{2,1,0:T(4,128)S(1)}, u32[]{:S(2)}, u32[]{:S(2)}) %collective-permute-start.5) | collective-permute-done | bytes 6176 | tf_op jit(solution)/shard_map/ppermute | solution.py:331
  220.8 1.9 collective-permute-start.6
  222.8 3.9 %collective-permute-start.7 = (f32[8,1,384]{2,1,0:T(1,128)S(1)}, f32[8,1,384]{2,1,0:T(1,128)S(1)}, u32[]{:S(2)}, u32[]{:S(2)}) collective-permute-start(f32[8,1,384]{2,1,0:T(1,128)S(1)} %get-tuple-element.12), channel_id=1, source_target_pairs={{0,1},{1,2},{2,3},{3,4},{4,5},{5,6},{6,7},{8,9},{9,10},{10,11},{11... | collective-permute-start | bytes 36872 | tf_op jit(solution)/shard_map/ppermute | solution.py:331
  226.7 12.5 %collective-permute-done.7 = f32[8,1,384]{2,1,0:T(1,128)S(1)} collective-permute-done((f32[8,1,384]{2,1,0:T(1,128)S(1)}, f32[8,1,384]{2,1,0:T(1,128)S(1)}, u32[]{:S(2)}, u32[]{:S(2)}) %collective-permute-start.7) | collective-permute-done | bytes 12320 | tf_op jit(solution)/shard_map/ppermute | solution.py:331
  239.5 1.9 collective-permute-start.8
  241.4 2.4 collective-permute-start.9
  243.9 5.8 %collective-permute-done.9 = f32[1,4,384]{2,1,0:T(4,128)S(1)} collective-permute-done((f32[1,4,384]{2,1,0:T(4,128)S(1)}, f32[1,4,384]{2,1,0:T(4,128)S(1)}, u32[]{:S(2)}, u32[]{:S(2)}) %collective-permute-start.9) | collective-permute-done | bytes 6176 | tf_op jit(solution)/shard_map/ppermute | solution.py:331
  249.7 1.9 collective-permute-start.10
  251.7 3.9 %collective-permute-start.11 = (f32[8,1,384]{2,1,0:T(1,128)S(1)}, f32[8,1,384]{2,1,0:T(1,128)S(1)}, u32[]{:S(2)}, u32[]{:S(2)}) collective-permute-start(f32[8,1,384]{2,1,0:T(1,128)S(1)} %get-tuple-element.10), channel_id=1, source_target_pairs={{0,1},{1,2},{2,3},{3,4},{4,5},{5,6},{6,7},{8,9},{9,10},{10,11},{11... | collective-permute-start | bytes 36872 | tf_op jit(solution)/shard_map/ppermute | solution.py:331
  255.6 12.5 %collective-permute-done.11 = f32[8,1,384]{2,1,0:T(1,128)S(1)} collective-permute-done((f32[8,1,384]{2,1,0:T(1,128)S(1)}, f32[8,1,384]{2,1,0:T(1,128)S(1)}, u32[]{:S(2)}, u32[]{:S(2)}) %collective-permute-start.11) | collective-permute-done | bytes 12320 | tf_op jit(solution)/shard_map/ppermute | solution.py:331
  (54 shorter events, 9.5 us)
Async XLA Ops:
  0.6 28.1 %copy-start = (bf16[2,384,384]{2,1,0:T(8,128)(2,1)S(1)}, bf16[2,384,384]{2,1,0:T(8,128)(2,1)}, u32[]{:S(2)}) copy-start(bf16[2,384,384]{2,1,0:T(8,128)(2,1)} %kspace_ref.1) | copy-start | bytes 1769476
  0.6 1.1 copy-start.2
  1.7 0.8 copy-start.7
  2.5 26.3 %copy-start.6 = (f32[2,384,24]{1,2,0:T(8,128)S(1)}, f32[2,384,24]{1,2,0:T(8,128)}, u32[]{:S(2)}) copy-start(f32[2,384,24]{1,2,0:T(8,128)} %param.14) | copy-start | bytes 221188
  2.5 26.3 %copy-start.8 = (s32[2,6,4]{1,2,0:T(4,128)S(1)}, s32[2,6,4]{1,2,0:T(4,128)}, u32[]{:S(2)}) copy-start(s32[2,6,4]{1,2,0:T(4,128)} %param.15) | copy-start | bytes 580
  28.7 0.7 copy-start.9
  29.4 1.0 copy-start.1
  30.5 1.0 copy-start.3
  31.4 1.0 copy-start.4
  32.4 1.0 copy-start.5
  153.9 0.6 copy-start.10
  172.4 9.2 %collective-permute-start.1 = (f32[1,4,384]{2,1,0:T(4,128)S(1)}, f32[1,4,384]{2,1,0:T(4,128)S(1)}, u32[]{:S(2)}, u32[]{:S(2)}) collective-permute-start(f32[1,4,384]{2,1,0:T(4,128)S(1)} %slice.163), channel_id=1, source_target_pairs={{0,8},{8,16},{16,24},{24,32},{32,40},{40,48},{48,56},{56,64},{64,7... | collective-permute-start | bytes 18440 | tf_op jit(solution)/shard_map/ppermute | solution.py:331
  174.7 8.2 %collective-permute-start = (f32[1,4,384]{2,1,0:T(4,128)S(1)}, f32[1,4,384]{2,1,0:T(4,128)S(1)}, u32[]{:S(2)}, u32[]{:S(2)}) collective-permute-start(f32[1,4,384]{2,1,0:T(4,128)S(1)} %slice.160), channel_id=1, source_target_pairs={{8,0},{16,8},{24,16},{32,24},{40,32},{48,40},{56,48},{64,56},{72,6... | collective-permute-start | bytes 18440 | tf_op jit(solution)/shard_map/ppermute | solution.py:333
  182.9 9.2 %collective-permute-start.2 = (f32[8,1,384]{2,1,0:T(1,128)S(1)}, f32[8,1,384]{2,1,0:T(1,128)S(1)}, u32[]{:S(2)}, u32[]{:S(2)}) collective-permute-start(f32[8,1,384]{2,1,0:T(1,128)S(1)} %get-tuple-element.15), channel_id=1, source_target_pairs={{1,0},{2,1},{3,2},{4,3},{5,4},{6,5},{7,6},{9,8},{10,9},{11,10},{12... | collective-permute-start | bytes 36872 | tf_op jit(solution)/shard_map/ppermute | solution.py:333
  190.1 16.5 %collective-permute-start.3 = (f32[8,1,384]{2,1,0:T(1,128)S(1)}, f32[8,1,384]{2,1,0:T(1,128)S(1)}, u32[]{:S(2)}, u32[]{:S(2)}) collective-permute-start(f32[8,1,384]{2,1,0:T(1,128)S(1)} %get-tuple-element.14), channel_id=1, source_target_pairs={{0,1},{1,2},{2,3},{3,4},{4,5},{5,6},{6,7},{8,9},{9,10},{10,11},{11... | collective-permute-start | bytes 36872 | tf_op jit(solution)/shard_map/ppermute | solution.py:331
  207.0 7.3 %collective-permute-start.4 = (f32[1,4,384]{2,1,0:T(4,128)S(1)}, f32[1,4,384]{2,1,0:T(4,128)S(1)}, u32[]{:S(2)}, u32[]{:S(2)}) collective-permute-start(f32[1,4,384]{2,1,0:T(4,128)S(1)} %get-tuple-element.19), channel_id=1, source_target_pairs={{8,0},{16,8},{24,16},{32,24},{40,32},{48,40},{56,48},{64,56},{72,6... | collective-permute-start | bytes 18440 | tf_op jit(solution)/shard_map/ppermute | solution.py:333
  212.4 8.4 %collective-permute-start.5 = (f32[1,4,384]{2,1,0:T(4,128)S(1)}, f32[1,4,384]{2,1,0:T(4,128)S(1)}, u32[]{:S(2)}, u32[]{:S(2)}) collective-permute-start(f32[1,4,384]{2,1,0:T(4,128)S(1)} %get-tuple-element.18), channel_id=1, source_target_pairs={{0,8},{8,16},{16,24},{24,32},{32,40},{40,48},{48,56},{56,64},{64,7... | collective-permute-start | bytes 18440 | tf_op jit(solution)/shard_map/ppermute | solution.py:331
  220.8 5.9 %collective-permute-start.6 = (f32[8,1,384]{2,1,0:T(1,128)S(1)}, f32[8,1,384]{2,1,0:T(1,128)S(1)}, u32[]{:S(2)}, u32[]{:S(2)}) collective-permute-start(f32[8,1,384]{2,1,0:T(1,128)S(1)} %get-tuple-element.13), channel_id=1, source_target_pairs={{1,0},{2,1},{3,2},{4,3},{5,4},{6,5},{7,6},{9,8},{10,9},{11,10},{12... | collective-permute-start | bytes 36872 | tf_op jit(solution)/shard_map/ppermute | solution.py:333
  222.8 16.4 %collective-permute-start.7 = (f32[8,1,384]{2,1,0:T(1,128)S(1)}, f32[8,1,384]{2,1,0:T(1,128)S(1)}, u32[]{:S(2)}, u32[]{:S(2)}) collective-permute-start(f32[8,1,384]{2,1,0:T(1,128)S(1)} %get-tuple-element.12), channel_id=1, source_target_pairs={{0,1},{1,2},{2,3},{3,4},{4,5},{5,6},{6,7},{8,9},{9,10},{10,11},{11... | collective-permute-start | bytes 36872 | tf_op jit(solution)/shard_map/ppermute | solution.py:331
  239.5 4.3 %collective-permute-start.8 = (f32[1,4,384]{2,1,0:T(4,128)S(1)}, f32[1,4,384]{2,1,0:T(4,128)S(1)}, u32[]{:S(2)}, u32[]{:S(2)}) collective-permute-start(f32[1,4,384]{2,1,0:T(4,128)S(1)} %get-tuple-element.17), channel_id=1, source_target_pairs={{8,0},{16,8},{24,16},{32,24},{40,32},{48,40},{56,48},{64,56},{72,6... | collective-permute-start | bytes 18440 | tf_op jit(solution)/shard_map/ppermute | solution.py:333
  241.4 8.3 %collective-permute-start.9 = (f32[1,4,384]{2,1,0:T(4,128)S(1)}, f32[1,4,384]{2,1,0:T(4,128)S(1)}, u32[]{:S(2)}, u32[]{:S(2)}) collective-permute-start(f32[1,4,384]{2,1,0:T(4,128)S(1)} %get-tuple-element.16), channel_id=1, source_target_pairs={{0,8},{8,16},{16,24},{24,32},{32,40},{40,48},{48,56},{56,64},{64,7... | collective-permute-start | bytes 18440 | tf_op jit(solution)/shard_map/ppermute | solution.py:331
  249.7 5.9 %collective-permute-start.10 = (f32[8,1,384]{2,1,0:T(1,128)S(1)}, f32[8,1,384]{2,1,0:T(1,128)S(1)}, u32[]{:S(2)}, u32[]{:S(2)}) collective-permute-start(f32[8,1,384]{2,1,0:T(1,128)S(1)} %get-tuple-element.11), channel_id=1, source_target_pairs={{1,0},{2,1},{3,2},{4,3},{5,4},{6,5},{7,6},{9,8},{10,9},{11,10},{12... | collective-permute-start | bytes 36872 | tf_op jit(solution)/shard_map/ppermute | solution.py:333
  251.7 16.4 %collective-permute-start.11 = (f32[8,1,384]{2,1,0:T(1,128)S(1)}, f32[8,1,384]{2,1,0:T(1,128)S(1)}, u32[]{:S(2)}, u32[]{:S(2)}) collective-permute-start(f32[8,1,384]{2,1,0:T(1,128)S(1)} %get-tuple-element.10), channel_id=1, source_target_pairs={{0,1},{1,2},{2,3},{3,4},{4,5},{5,6},{6,7},{8,9},{9,10},{10,11},{11... | collective-permute-start | bytes 36872 | tf_op jit(solution)/shard_map/ppermute | solution.py:331

commit v2 on v1

v2 whole, which is shorter than its diff:
```python
import functools
import math

import jax
import jax.numpy as jnp
import numpy as np
from jax import lax
from jax.experimental import pallas as pl
from jax.experimental.pallas import tpu as pltpu
from jax.sharding import PartitionSpec as P

SHOTS = 6
TAPS = 8
DIFF_STEPS = 3
COILS = 16
WIDE = 64
NARROW = 8
LINES = 384
COLS = 24
ROWS = 6
SLICES = 4
READOUT = 384
SPAN = 512
PIECES = 3
EDGE = DIFF_STEPS
PLACES = ROWS + 2 * EDGE
DENSE = 5
HALO = 24
BAND_BITS = 5

penalty = 0.5
time_step = 0.18
axis_weights = (1.0, 0.5, 1.0)

F32 = jnp.float32
BF16 = jnp.bfloat16
MESH = pl.DeviceIdType.MESH


def cosine_table():
    freq = np.arange(LINES, dtype=np.float32)[:, None]
    cell = np.arange(LINES, dtype=np.float32)[None, :]
    angle = np.float32(math.pi) * (cell + np.float32(0.5)) * freq / np.float32(LINES)
    entries = np.cos(angle).astype(np.float32) * np.float32(math.sqrt(2.0 / LINES))
    entries = entries * np.where(freq == 0.0, np.float32(math.sqrt(0.5)), np.float32(1.0))
    return entries.astype(np.float32)


def place_tables():
    place = np.zeros((WIDE * 8, LINES + 128), np.float32)
    for w in range(WIDE):
        for i in range(ROWS):
            place[8 * w + i, ROWS * w + i] = 1.0
        for g in range(2):
            place[8 * w + 6 + g, LINES + g * 64 + w] = 1.0
    order = np.zeros((3 * 128, LINES), np.float32)
    for t in range(3):
        for g in range(2):
            for w in range(WIDE):
                order[t * 128 + g * 64 + w, ROWS * w + 3 * g + t] = 1.0
    return place, order


def return_tables():
    spread = np.zeros((PLACES * WIDE, LINES), np.float32)
    for i in range(PLACES):
        for w in range(WIDE):
            line = ROWS * w - EDGE + i
            if 0 <= line < LINES:
                spread[i * WIDE + w, line] = 1.0
    rep = np.zeros((128, 2 * READOUT), np.float32)
    for i in range(2):
        for x in range(READOUT):
            rep[48 * i + x % COLS, i * READOUT + x] = 1.0
    pick = np.zeros((SLICES * 16, 2 * 6 * WIDE), np.float32)
    for i in range(2):
        for m in range(6):
            for w in range(WIDE):
                pick[(w // 16) * 16 + 2 * m + i, (i * 6 + m) * WIDE + w] = 1.0
    return spread, rep, pick


def lane_iota(rows, lanes):
    return lax.broadcasted_iota(jnp.int32, (rows, lanes), 1)


def poly_sin(x):
    x2 = x * x
    return x * (1.0 + x2 * (-1.0 / 6 + x2 * (1.0 / 120 + x2 * (-1.0 / 5040 + x2 * (1.0 / 362880)))))


def poly_cos(x):
    x2 = x * x
    return 1.0 + x2 * (-0.5 + x2 * (1.0 / 24 + x2 * (-1.0 / 720 + x2 * (1.0 / 40320 - x2 * (1.0 / 3628800)))))


def tap_weights(frac):
    near = jnp.minimum(frac, 1.0 - frac) * (math.pi / 2)
    full = 2.0 * poly_sin(near) * poly_cos(near)
    phi = frac * (math.pi / 4)
    sin_a, cos_a = poly_sin(phi), poly_cos(phi)
    rest = (1.0 - frac) * (math.pi / 4)
    sin_b, cos_b = poly_sin(rest), poly_cos(rest)
    quarter = {-3: -sin_b, -2: -cos_a, -1: -cos_b, 0: -sin_a, 1: sin_b, 2: cos_a, 3: cos_b, 4: sin_a}
    weights = []
    for k in range(TAPS):
        n = k - 3
        t = n - frac
        sign = 1.0 if n % 2 else -1.0
        if n in (0, 1):
            small = jnp.abs(t) < 1e-5
            inverse = 1.0 / jnp.where(small, 1.0, t)
            product = (full * inverse) * (quarter[n] * inverse) * (sign * 4.0 / math.pi**2)
            weights.append(jnp.where(small, 1.0, product))
        else:
            inverse = 1.0 / t
            weights.append((full * inverse) * (quarter[n] * inverse) * (sign * 4.0 / math.pi**2))
    return weights


def wide_lines(values):
    return jnp.concatenate([values, jnp.zeros((values.shape[0], SPAN - LINES), F32)], axis=1)


def left(values, count):
    return pltpu.roll(values, (SPAN - count) % SPAN, 1) if count % SPAN else values


def split3(values):
    high = values.astype(BF16)
    rest = values - high.astype(F32)
    middle = rest.astype(BF16)
    low = (rest - middle.astype(F32)).astype(BF16)
    return high, middle, low


def dot(a, b):
    return jnp.dot(a, b, preferred_element_type=F32)


def dot_first(a, b):
    return lax.dot_general(a, b, (((0,), (0,)), ((), ())), preferred_element_type=F32)


def step_scalars(rr, ra, aa, ab):
    alpha = rr / (penalty * rr + ra)
    rho = ra / rr
    qq = jnp.maximum(aa - rho * ra, 0.0)
    qaq = ab - 2.0 * rho * aa + rho * rho * ra
    next_rr = alpha * alpha * qq
    beta = next_rr / rr
    direction_sq = next_rr + beta * beta * rr
    direction_a = alpha * alpha * qaq - 2.0 * beta * alpha * qq + beta * beta * ra
    image = jnp.maximum(penalty * direction_sq + direction_a, penalty * direction_sq)
    second = jnp.where(image > 0.0, next_rr / jnp.where(image > 0.0, image, 1.0), 0.0)
    return alpha + second * (alpha * rho + beta), -second * alpha


def whole_body(
    prior_ref, maps_ref, start_ref, mask_ref, kspace_any, frac_any, table_any, turned_any, place_any, order_any,
    spread_any, rep_any, pick_any,
    solution_ref, denoised_ref,
    kspace_ref, frac_ref, table_ref, turned_ref, place_ref, order_ref, spread_ref, rep_ref, pick_ref,
    send_maps, got_ref, edge_ref, maps3_ref, weight_ref, data_ref, start_rows_ref,
    send_fields, got_fields, near_sum, far_sum, send_halo, got_halo,
    load_sem, maps_sem, edge_send, edge_recv, field_sem, near_sem, far_sem, halo_send, halo_recv,
):
    me = lax.axis_index("wide")
    nme = lax.axis_index("narrow")
    my_slice = me // 16
    both = 2 * COLS
    barrier = pltpu.get_barrier_semaphore()

    @pl.loop(1, WIDE)
    def _(k):
        pl.semaphore_signal(barrier, inc=1, device_id={"wide": lax.rem(me + k, WIDE)}, device_id_type=MESH)

    @pl.loop(1, NARROW)
    def _(k):
        pl.semaphore_signal(barrier, inc=1, device_id={"narrow": lax.rem(nme + k, NARROW)}, device_id_type=MESH)

    sources = (kspace_any, frac_any, table_any, turned_any, place_any, order_any, spread_any, rep_any, pick_any)
    targets = (kspace_ref, frac_ref, table_ref, turned_ref, place_ref, order_ref, spread_ref, rep_ref, pick_ref)
    loads = [pltpu.make_async_copy(a, b, load_sem.at[i]) for i, (a, b) in enumerate(zip(sources, targets))]
    for load in loads:
        load.start()

    lane8 = lane_iota(8, 128)
    stacked = [jnp.concatenate([prior_ref[t], prior_ref[3 + t]], axis=0) for t in range(3)]
    for q in range(16):
        packed = jnp.zeros((8, 128), F32)
        for t in range(3):
            turned = pltpu.roll(stacked[t], (24 * t - 24 * q) % READOUT, 1)[:, :128]
            packed = jnp.where((lane8 >= 24 * t) & (lane8 < 24 * t + 24), turned, packed)
        high = packed.astype(BF16).astype(F32)
        rest = packed - high
        middle = rest.astype(BF16).astype(F32)
        low = rest - middle
        packed = jnp.concatenate([high, middle, low], axis=1)
        for s in range(SLICES):
            d = 16 * s + q
            block = maps_ref[:, d * 384 : (d + 1) * 384].astype(F32)
            message = jnp.concatenate([block, packed[s : s + 1], packed[4 + s : 5 + s]], axis=0)
            send_maps[d] = message.astype(BF16)

    pl.semaphore_wait(barrier, WIDE + NARROW - 2)

    def to_wide(k, source, target, sems):
        to = lax.rem(me + k, WIDE)
        pltpu.make_async_remote_copy(
            src_ref=source(to), dst_ref=target, send_sem=sems.at[0], recv_sem=sems.at[1],
            device_id={"wide": to}, device_id_type=MESH,
        ).start()

    def finish(source, target, sems, count):
        others = pl.ds(0, count)
        pltpu.make_async_copy(source.at[others], source.at[others], sems.at[0]).wait()
        pltpu.make_async_copy(target.at[others], target.at[others], sems.at[1]).wait()

    @pl.loop(1, WIDE)
    def _(k):
        to_wide(k, lambda to: send_maps.at[to], got_ref.at[me], maps_sem)

    got_ref[me] = send_maps[me]

    edges = [
        pltpu.make_async_remote_copy(
            src_ref=prior_ref.at[pl.ds(first, EDGE)], dst_ref=edge_ref.at[side],
            send_sem=edge_send.at[side], recv_sem=edge_recv.at[side],
            device_id={"wide": lax.rem(me + step, WIDE)}, device_id_type=MESH,
        )
        for side, first, step in ((0, ROWS - EDGE, 1), (1, 0, WIDE - 1))
    ]
    for edge in edges:
        edge.start()

    starts = []
    diagonal = lax.broadcasted_iota(jnp.int32, (COLS, COLS), 0) == lax.broadcasted_iota(jnp.int32, (COLS, COLS), 1)
    for p in range(2):
        row = jnp.broadcast_to(start_ref[p : p + 1, :].astype(F32), (COLS, COLS))
        starts.append(jnp.sum(jnp.where(diagonal, row, 0.0), axis=1, keepdims=True))
    ahead = jnp.concatenate(starts, axis=0).astype(jnp.int32) + 12
    start_rows_ref[...] = jnp.broadcast_to(ahead, (both, SPAN))

    loads[1].wait()
    frac = jnp.concatenate([frac_ref[0], frac_ref[1]], axis=0)
    for k, weight in enumerate(tap_weights(frac)):
        weight_ref[k] = weight

    shot = lax.rem(lane_iota(1, LINES), SHOTS)
    masks = []
    for p in range(2):
        row = jnp.zeros((1, LINES), F32)
        for h in range(SHOTS):
            row = jnp.where(shot == h, mask_ref[p, my_slice, h].astype(F32), row)
        masks.append(row)
    loads[3].wait()
    turned = turned_ref[...].astype(F32)
    forward = [(turned * masks[p]).astype(BF16) for p in range(2)]
    loads[0].wait()
    for p in range(2):
        data_ref[p] = lax.dot_general(
            kspace_ref[p], forward[p], (((0,), (1,)), ((), ())), preferred_element_type=F32
        )
    for i in (2, 4, 5, 6, 7, 8):
        loads[i].wait()

    finish(send_maps, got_ref, maps_sem, WIDE - 1)
    got = got_ref[...].reshape(WIDE * 8, LINES)
    laid = dot_first(got, place_ref[...])
    maps3_ref[...] = laid[:, :LINES].reshape(COLS, COILS, LINES)
    pieces = []
    for m in range(PIECES):
        parts = [laid[m * 128 + 24 * t : m * 128 + 24 * t + 24, LINES:] for t in range(3)]
        pieces.append(jnp.concatenate(parts, axis=1))
    ordered = dot(jnp.concatenate(pieces, axis=0).astype(BF16), order_ref[...])
    prior = ordered[:COLS] + ordered[COLS : 2 * COLS] + ordered[2 * COLS :]

    def bit_set(bit):
        return ((start_rows_ref[...] >> bit) & 1) == 1

    def band_apply(field):
        value = wide_lines(jnp.concatenate([field, field], axis=0))
        value = left(value, -15)
        for bit in range(BAND_BITS):
            value = jnp.where(bit_set(bit), left(value, 1 << bit), value)
        total = jnp.zeros((both, LINES), F32)
        for k in range(TAPS):
            total = total + weight_ref[k] * left(value, k)[:, :LINES]
        return total

    def band_adjoint(values):
        total = jnp.zeros((both, SPAN), F32)
        for k in range(TAPS):
            total = total + left(wide_lines(weight_ref[k] * values), -k)
        for bit in range(BAND_BITS):
            total = jnp.where(bit_set(bit), left(total, -(1 << bit)), total)
        total = left(total, 15)
        return (total[:COLS] + total[COLS:])[:, :LINES]

    def spectra(moved, p):
        image = maps3_ref[...] * moved[p * COLS : (p + 1) * COLS][:, None, :]
        return dot(image.reshape(COLS * COILS, LINES).astype(BF16), forward[p])

    def combine(back):
        return jnp.sum(back.reshape(COLS, COILS, LINES) * maps3_ref[...], axis=1)

    def through(field):
        moved = band_apply(field)
        return [dot(spectra(moved, p).astype(BF16), table_ref[...]) for p in range(2)]

    back = through(prior)
    residue = band_adjoint(jnp.concatenate([combine(data_ref[p] - back[p]) for p in range(2)], axis=0))
    back = through(residue)
    first = band_adjoint(jnp.concatenate([combine(back[p]) for p in range(2)], axis=0))

    fields = jnp.concatenate([residue, first, jnp.zeros((128 - 2 * COLS, LINES), F32)], axis=0)
    high = fields.astype(BF16)
    low = (fields - high.astype(F32)).astype(BF16)
    across = (((1,), (1,)), ((), ()))
    placed = lax.dot_general(spread_ref[...], high, across, preferred_element_type=F32)
    placed = placed + lax.dot_general(spread_ref[...], low, across, preferred_element_type=F32)
    lane = lane_iota(WIDE, 128)
    for row in range(DENSE):
        packed = jnp.zeros((WIDE, 128), F32)
        for i in range(PLACES):
            begin = 48 * i - 128 * row
            if begin < 128 and begin + 48 > 0:
                turned = placed[i * WIDE : (i + 1) * WIDE]
                if begin % 128:
                    turned = pltpu.roll(turned, begin % 128, 1)
                packed = jnp.where((lane >= begin) & (lane < begin + 48), turned, packed)
        send_fields[:, row, :] = packed

    @pl.loop(1, WIDE)
    def _(k):
        to_wide(k, lambda to: send_fields.at[to], got_fields.at[me], field_sem)

    got_fields[me] = send_fields[me]

    moved = band_apply(first)
    squares = jnp.zeros((1, LINES), F32)
    for p in range(2):
        here = spectra(moved, p)
        squares = squares + jnp.sum(here * here.astype(BF16).astype(F32), axis=0, keepdims=True)

    def total(values):
        return jnp.sum(jnp.sum(values, axis=0, keepdims=True), axis=1, keepdims=True)

    lane1 = lane_iota(1, 128)
    sums = jnp.zeros((1, 128), F32)
    for i, part in enumerate((residue * residue, residue * first, first * first, squares)):
        sums = jnp.where(lane1 == i, total(part), sums)
    near_sum[nme] = sums

    @pl.loop(1, NARROW)
    def _(k):
        to = lax.rem(nme + k, NARROW)
        pltpu.make_async_remote_copy(
            src_ref=near_sum.at[nme], dst_ref=near_sum.at[nme], send_sem=near_sem.at[0], recv_sem=near_sem.at[1],
            device_id={"narrow": to}, device_id_type=MESH,
        ).start()

    for edge in edges:
        edge.wait()
    below = jnp.where(me > 0, 1.0, 0.0).astype(F32)
    above = jnp.where(me < WIDE - 1, 1.0, 0.0).astype(F32)
    cells = []
    for s in range(SLICES):
        rows = [edge_ref[0, i, s : s + 1, :] * below for i in range(EDGE)]
        rows += [prior_ref[i, s : s + 1, :] for i in range(ROWS)]
        rows += [edge_ref[1, i, s : s + 1, :] * above for i in range(EDGE)]
        rows += [jnp.zeros((16 - PLACES, READOUT), F32)]
        cells.append(jnp.concatenate(rows, axis=0))

    finish(near_sum, near_sum, near_sem, NARROW - 1)
    far_sum[me] = jnp.sum(near_sum[...].reshape(NARROW, 128), axis=0, keepdims=True)

    @pl.loop(1, WIDE)
    def _(k):
        to_wide(k, lambda to: far_sum.at[me], far_sum.at[me], far_sem)

    finish(far_sum, far_sum, far_sem, WIDE - 1)
    sums = jnp.sum(far_sum[...].reshape(WIDE, 128), axis=0, keepdims=True)
    picked = [jnp.sum(jnp.where(lane1 == i, sums, 0.0), axis=1, keepdims=True) for i in range(4)]
    c0, c1 = step_scalars(*picked)
    solution_ref[...] = prior + c0 * residue + c1 * first

    finish(send_fields, got_fields, field_sem, WIDE - 1)
    lines = [got_fields[:, row, :] for row in range(DENSE)]
    pairs = []
    for m in range(6):
        begin = 96 * m
        row, off = begin // 128, begin % 128
        pair = pltpu.roll(lines[row], 128 - off, 1) if off else lines[row]
        if off + 96 > 128:
            pair = jnp.where(lane < 128 - off, pair, pltpu.roll(lines[row + 1], 128 - off, 1))
        pairs.append(pair)
    pairs = jnp.concatenate(pairs, axis=0)
    joined = c0 * pairs + c1 * pltpu.roll(pairs, 128 - COLS, 1)
    high = joined.astype(BF16)
    low = (joined - high.astype(F32)).astype(BF16)
    block_of = lax.broadcasted_iota(jnp.int32, (16, 2 * READOUT), 0)
    readout_of = lax.rem(lane_iota(16, 2 * READOUT), READOUT)
    inside = (readout_of >= COLS * block_of) & (readout_of < COLS * block_of + COLS)
    change = jnp.zeros((SLICES * 16, READOUT), F32)
    for part in (high, low):
        wide = dot(part, rep_ref[...]).reshape(6 * SLICES, 16, 2 * READOUT)
        wide = jnp.where(inside[None], wide, 0.0).reshape(6 * WIDE, 2 * READOUT).astype(BF16)
        wide = jnp.concatenate([wide[:, :READOUT], wide[:, READOUT:]], axis=0)
        change = change + dot(pick_ref[...], wide)
    cells = [cells[s] + change[16 * s : 16 * s + 16] for s in range(SLICES)]

    def diamond(near, middle, far):
        rows = jnp.concatenate([near[1:11], middle[2:10], far[3:9]], axis=0)
        return rows.astype(BF16)

    send_halo[0] = diamond(cells[3], cells[2], cells[1])
    send_halo[1] = diamond(cells[0], cells[1], cells[2])
    halos = [
        pltpu.make_async_remote_copy(
            src_ref=send_halo.at[side], dst_ref=got_halo.at[side],
            send_sem=halo_send.at[side], recv_sem=halo_recv.at[side],
            device_id={"narrow": lax.rem(nme + step, NARROW)}, device_id_type=MESH,
        )
        for side, step in ((0, 1), (1, NARROW - 1))
    ]
    for halo in halos:
        halo.start()
    for halo in halos:
        halo.wait()

    def opened(side, keep):
        rows = got_halo[side].astype(F32) * keep
        zero = jnp.zeros((8, READOUT), F32)
        near = jnp.concatenate([zero[:1], rows[:10], zero[:5]], axis=0)
        middle = jnp.concatenate([zero[:2], rows[10:18], zero[:6]], axis=0)
        far = jnp.concatenate([zero[:3], rows[18:24], zero[:7]], axis=0)
        return near, middle, far

    has_low = jnp.where(nme > 0, 1.0, 0.0).astype(F32)
    has_high = jnp.where(nme < NARROW - 1, 1.0, 0.0).astype(F32)
    near_low, mid_low, far_low = opened(0, has_low)
    near_high, mid_high, far_high = opened(1, has_high)
    volume = [far_low, mid_low, near_low] + cells + [near_high, mid_high, far_high]
    keeps = [has_low] * 3 + [None] * SLICES + [has_high] * 3
    margin = jnp.zeros((16, 128), F32)
    volume = [jnp.concatenate([one, margin], axis=1) for one in volume]
    line_of = lax.broadcasted_iota(jnp.int32, (16, READOUT + 128), 0) + (ROWS * me - EDGE)
    in_grid = (line_of >= 0) & (line_of < LINES) & (lane_iota(16, READOUT + 128) < READOUT)
    in_grid = in_grid.astype(F32)

    def flux(jump):
        return jump / (1.0 + jump * jump)

    for step in range(DIFF_STEPS):
        last = len(volume) - 1
        across_slices = [flux(volume[i + 1] - volume[i]) for i in range(last)]
        after = []
        for i in range(1, last):
            one = volume[i]
            down = flux(pltpu.roll(one, 15, 0) - one)
            along = flux(pltpu.roll(one, SPAN - 1, 1) - one)
            moved = axis_weights[0] * (down - pltpu.roll(down, 1, 0))
            moved = moved + axis_weights[1] * (across_slices[i] - across_slices[i - 1])
            moved = moved + axis_weights[2] * (along - pltpu.roll(along, 1, 1))
            grid = in_grid if keeps[i] is None else in_grid * keeps[i]
            after.append((one + time_step * moved) * grid)
        volume = after
        keeps = keeps[1:-1]
    for s in range(SLICES):
        for i in range(ROWS):
            denoised_ref[i, s : s + 1, :] = volume[s][EDGE + i : EDGE + i + 1, :READOUT]


def whole(prior, coil_maps, kspace, band_start, frac, mask):
    vmem = pl.BlockSpec(memory_space=pltpu.VMEM)
    smem = pl.BlockSpec(memory_space=pltpu.SMEM)
    far = pl.BlockSpec(memory_space=pl.ANY)
    table = cosine_table()
    constants = (table, table.T) + place_tables() + return_tables()
    constants = [jnp.asarray(one, BF16) for one in constants]
    moved = [kspace, frac] + constants
    return pl.pallas_call(
        whole_body,
        out_shape=(
            jax.ShapeDtypeStruct((COLS, LINES), F32),
            jax.ShapeDtypeStruct((ROWS, SLICES, READOUT), F32),
        ),
        in_specs=[vmem, vmem, vmem, smem] + [far] * len(moved),
        out_specs=(vmem, vmem),
        scratch_shapes=[pltpu.VMEM(one.shape, one.dtype) for one in moved]
        + [
            pltpu.VMEM((WIDE, 8, LINES), BF16),
            pltpu.VMEM((WIDE, 8, LINES), BF16),
            pltpu.VMEM((2, EDGE, SLICES, READOUT), F32),
            pltpu.VMEM((COLS, COILS, LINES), F32),
            pltpu.VMEM((TAPS, 2 * COLS, LINES), F32),
            pltpu.VMEM((2, COLS * COILS, LINES), F32),
            pltpu.VMEM((2 * COLS, SPAN), jnp.int32),
            pltpu.VMEM((WIDE, DENSE, 128), F32),
            pltpu.VMEM((WIDE, DENSE, 128), F32),
            pltpu.VMEM((NARROW, 1, 128), F32),
            pltpu.VMEM((WIDE, 1, 128), F32),
            pltpu.VMEM((2, HALO, READOUT), BF16),
            pltpu.VMEM((2, HALO, READOUT), BF16),
            pltpu.SemaphoreType.DMA((len(moved),)),
            pltpu.SemaphoreType.DMA((2,)),
            pltpu.SemaphoreType.DMA((2,)),
            pltpu.SemaphoreType.DMA((2,)),
            pltpu.SemaphoreType.DMA((2,)),
            pltpu.SemaphoreType.DMA((2,)),
            pltpu.SemaphoreType.DMA((2,)),
            pltpu.SemaphoreType.DMA((2,)),
            pltpu.SemaphoreType.DMA((2,)),
        ],
        compiler_params=pltpu.CompilerParams(collective_id=0, has_side_effects=True, vmem_limit_bytes=48 << 20),
        name="whole",
    )(prior, coil_maps, band_start, mask, *moved)


def per_device(prior, coil_maps, kspace, band_start, band_frac, shot_mask):
    solved, denoised = whole(
        prior, coil_maps, kspace, band_start, jnp.transpose(band_frac, (0, 2, 1)), jnp.transpose(shot_mask, (0, 2, 1))
    )
    return jnp.transpose(solved), denoised


def solution(mesh):
    in_specs = (
        P("wide", "narrow", None),
        P("wide", "narrow"),
        P(None, None, ("narrow", "wide")),
        P(None, ("narrow", "wide")),
        P(None, None, ("narrow", "wide")),
        P(None, None, "narrow"),
    )
    out_specs = (P(None, ("narrow", "wide")), P("wide", "narrow", None))
    return jax.shard_map(per_device, mesh=mesh, in_specs=in_specs, out_specs=out_specs, check_vma=False)
```

time: 270 us -> 89.1 us (0.33)
  the two profiles are of different devices: /device:TPU:384 before, /device:TPU:1 now
where the time goes in v2:
time: 89.1 us; the launch traced here: 88.5 us
  Pallas kernels  74.7 us (84%)
  local copies, waits for them, and re-layouts  13.1 us (15%)
    pallas_call x1, Pallas kernels, whole(): pl.pallas_call(whole_body, out_shape=(jax.ShapeDtypeStruct((COLS, LINES),...  74.7 us
    unnamed x28, local copies, waits for them, and re-layouts  13.1 us

profile of v2, /device:TPU:1, one launch (start us, length us, event | category | flops | bytes accessed | tf_op | source)
XLA Modules:
  0.0 88.5 jit_solution(11686687423246981047)
XLA Ops:
  0.6 0.0 copy-start.12
  0.6 0.7 copy-done.12
  1.3 0.0 copy-start
  1.3 1.1 %copy-done = bf16[2,384,384]{2,1,0:T(8,128)(2,1)S(1)} copy-done((bf16[2,384,384]{2,1,0:T(8,128)(2,1)S(1)}, bf16[2,384,384]{2,1,0:T(8,128)(2,1)}, u32[]{:S(2)}) %copy-start) | copy-done | bytes 589848
  2.4 0.0 copy-start.1
  2.4 1.1 %copy-done.1 = bf16[768,384]{1,0:T(8,128)(2,1)S(1)} copy-done((bf16[768,384]{1,0:T(8,128)(2,1)S(1)}, bf16[768,384]{1,0:T(8,128)(2,1)}, u32[]{:S(2)}) %copy-start.1) | copy-done | bytes 589848
  3.4 0.0 copy-start.2
  3.4 1.0 %copy-done.2 = bf16[512,512]{1,0:T(8,128)(2,1)S(1)} copy-done((bf16[512,512]{1,0:T(8,128)(2,1)S(1)}, bf16[512,512]{1,0:T(8,128)(2,1)}, u32[]{:S(2)}) %copy-start.2) | copy-done | bytes 524312
  4.5 0.0 copy-start.3
  4.5 1.0 %copy-done.3 = bf16[6,24576]{1,0:T(8,128)(2,1)S(1)} copy-done((bf16[6,24576]{1,0:T(8,128)(2,1)S(1)}, bf16[6,24576]{1,0:T(8,128)(2,1)}, u32[]{:S(2)}) %copy-start.3) | copy-done | bytes 294936
  5.5 0.0 copy-start.4
  5.5 1.0 %copy-done.4 = bf16[384,384]{1,0:T(8,128)(2,1)S(1)} copy-done((bf16[384,384]{1,0:T(8,128)(2,1)S(1)}, bf16[384,384]{1,0:T(8,128)(2,1)}, u32[]{:S(2)}) %copy-start.4) | copy-done | bytes 294936
  6.4 0.0 copy-start.5
  6.4 1.0 %copy-done.5 = bf16[384,384]{1,0:T(8,128)(2,1)S(1)} copy-done((bf16[384,384]{1,0:T(8,128)(2,1)S(1)}, bf16[384,384]{1,0:T(8,128)(2,1)}, u32[]{:S(2)}) %copy-start.5) | copy-done | bytes 294936
  7.4 0.0 copy-start.6
  7.4 1.0 %copy-done.6 = bf16[384,384]{1,0:T(8,128)(2,1)S(1)} copy-done((bf16[384,384]{1,0:T(8,128)(2,1)S(1)}, bf16[384,384]{1,0:T(8,128)(2,1)}, u32[]{:S(2)}) %copy-start.6) | copy-done | bytes 294936
  8.4 0.9 %copy-done.7 = bf16[128,768]{1,0:T(8,128)(2,1)S(1)} copy-done((bf16[128,768]{1,0:T(8,128)(2,1)S(1)}, bf16[128,768]{1,0:T(8,128)(2,1)}, u32[]{:S(2)}) %copy-start.7) | copy-done | bytes 196632
  9.3 0.9 %copy-done.8 = bf16[64,768]{1,0:T(8,128)(2,1)S(1)} copy-done((bf16[64,768]{1,0:T(8,128)(2,1)S(1)}, bf16[64,768]{1,0:T(8,128)(2,1)}, u32[]{:S(2)}) %copy-start.8) | copy-done | bytes 98328
  10.2 0.9 copy-done.9
  11.1 0.8 copy-done.10
  11.8 0.7 copy-done.11
  12.5 74.7 %whole.1 = (f32[24,384]{1,0:T(8,128)S(1)}, f32[6,4,384]{2,1,0:T(4,128)S(1)}) custom-call(f32[6,4,384]{2,1,0:T(4,128)S(1)} %copy-done.10, bf16[6,24576]{1,0:T(8,128)(2,1)S(1)} %copy-done.3, s32[2,24]{1,0:T(2,128)S(1)} %copy-done.12, s32[2,4,6]{2,1,0:T(4,128)S(1)} %bitcast.5, bf16[2,384,384]{2,1,0:T(8,128)(2,1)S(1)} %copy-done, f32[2,24,384]{2,1,0:T(8,128)S(1)} %bitcast.3, ...), custom_call_target="tpu_custom_call" | custom-call | tf_op jit(solution)/shard_map/whole/pallas_call | solution.py:484
  87.3 0.6 copy.17
  87.9 0.6 copy.18
  (5 shorter events, 0.0 us)
Async XLA Ops:
  0.6 0.7 copy-start.12
  1.3 1.1 %copy-start = (bf16[2,384,384]{2,1,0:T(8,128)(2,1)S(1)}, bf16[2,384,384]{2,1,0:T(8,128)(2,1)}, u32[]{:S(2)}) copy-start(bf16[2,384,384]{2,1,0:T(8,128)(2,1)} %kspace_any.1) | copy-start | bytes 1769476
  2.4 1.1 %copy-start.1 = (bf16[768,384]{1,0:T(8,128)(2,1)S(1)}, bf16[768,384]{1,0:T(8,128)(2,1)}, u32[]{:S(2)}) copy-start(bf16[768,384]{1,0:T(8,128)(2,1)} %constant.18.clone.spread_any) | copy-start | bytes 1769476
  3.4 1.0 %copy-start.2 = (bf16[512,512]{1,0:T(8,128)(2,1)S(1)}, bf16[512,512]{1,0:T(8,128)(2,1)}, u32[]{:S(2)}) copy-start(bf16[512,512]{1,0:T(8,128)(2,1)} %constant.16.clone.place_any) | copy-start | bytes 1572868
  4.5 1.0 %copy-start.3 = (bf16[6,24576]{1,0:T(8,128)(2,1)S(1)}, bf16[6,24576]{1,0:T(8,128)(2,1)}, u32[]{:S(2)}) copy-start(bf16[6,24576]{1,0:T(8,128)(2,1)} %maps_ref.1) | copy-start | bytes 884740
  5.5 1.0 %copy-start.4 = (bf16[384,384]{1,0:T(8,128)(2,1)S(1)}, bf16[384,384]{1,0:T(8,128)(2,1)}, u32[]{:S(2)}) copy-start(bf16[384,384]{1,0:T(8,128)(2,1)} %constant.17.clone.order_any) | copy-start | bytes 884740
  6.4 1.0 %copy-start.5 = (bf16[384,384]{1,0:T(8,128)(2,1)S(1)}, bf16[384,384]{1,0:T(8,128)(2,1)}, u32[]{:S(2)}) copy-start(bf16[384,384]{1,0:T(8,128)(2,1)} %constant.15.clone.turned_any) | copy-start | bytes 884740
  7.4 1.0 %copy-start.6 = (bf16[384,384]{1,0:T(8,128)(2,1)S(1)}, bf16[384,384]{1,0:T(8,128)(2,1)}, u32[]{:S(2)}) copy-start(bf16[384,384]{1,0:T(8,128)(2,1)} %constant.14.clone.table_any) | copy-start | bytes 884740
  8.4 0.9 %copy-start.7 = (bf16[128,768]{1,0:T(8,128)(2,1)S(1)}, bf16[128,768]{1,0:T(8,128)(2,1)}, u32[]{:S(2)}) copy-start(bf16[128,768]{1,0:T(8,128)(2,1)} %constant.19.clone.rep_any) | copy-start | bytes 589828
  9.3 0.9 %copy-start.8 = (bf16[64,768]{1,0:T(8,128)(2,1)S(1)}, bf16[64,768]{1,0:T(8,128)(2,1)}, u32[]{:S(2)}) copy-start(bf16[64,768]{1,0:T(8,128)(2,1)} %constant.20.clone.pick_any) | copy-start | bytes 294916
  10.2 0.9 copy-start.9
  11.1 0.8 copy-start.10
  11.8 0.7 copy-start.11

commit v3 on v2

--- a/solution.py
+++ b/solution.py
@@ -157,10 +157,11 @@
 
 
 def whole_body(
-    prior_ref, maps_ref, start_ref, mask_ref, kspace_any, frac_any, table_any, turned_any, place_any, order_any,
-    spread_any, rep_any, pick_any,
+    mask_any, kspace_any, frac_any, table_any, turned_any, place_any, order_any,
+    spread_any, rep_any, pick_any, prior_any, maps_any, start_any,
     solution_ref, denoised_ref,
-    kspace_ref, frac_ref, table_ref, turned_ref, place_ref, order_ref, spread_ref, rep_ref, pick_ref,
+    mask_ref, kspace_ref, frac_ref, table_ref, turned_ref, place_ref, order_ref, spread_ref, rep_ref, pick_ref,
+    prior_ref, maps_ref, start_ref,
     send_maps, got_ref, edge_ref, maps3_ref, weight_ref, data_ref, start_rows_ref,
     send_fields, got_fields, near_sum, far_sum, send_halo, got_halo,
     load_sem, maps_sem, edge_send, edge_recv, field_sem, near_sem, far_sem, halo_send, halo_recv,
@@ -171,6 +172,18 @@
     both = 2 * COLS
     barrier = pltpu.get_barrier_semaphore()
 
+    sources = (
+        kspace_any, frac_any, table_any, turned_any, place_any, order_any, spread_any, rep_any, pick_any,
+        prior_any, maps_any, start_any, mask_any,
+    )
+    targets = (
+        kspace_ref, frac_ref, table_ref, turned_ref, place_ref, order_ref, spread_ref, rep_ref, pick_ref,
+        prior_ref, maps_ref, start_ref, mask_ref,
+    )
+    loads = [pltpu.make_async_copy(a, b, load_sem.at[i]) for i, (a, b) in enumerate(zip(sources, targets))]
+    for i in (9, 10, 11, 12, 1, 3, 0, 2, 4, 5, 6, 7, 8):
+        loads[i].start()
+
     @pl.loop(1, WIDE)
     def _(k):
         pl.semaphore_signal(barrier, inc=1, device_id={"wide": lax.rem(me + k, WIDE)}, device_id_type=MESH)
@@ -179,12 +192,9 @@
     def _(k):
         pl.semaphore_signal(barrier, inc=1, device_id={"narrow": lax.rem(nme + k, NARROW)}, device_id_type=MESH)
 
-    sources = (kspace_any, frac_any, table_any, turned_any, place_any, order_any, spread_any, rep_any, pick_any)
-    targets = (kspace_ref, frac_ref, table_ref, turned_ref, place_ref, order_ref, spread_ref, rep_ref, pick_ref)
-    loads = [pltpu.make_async_copy(a, b, load_sem.at[i]) for i, (a, b) in enumerate(zip(sources, targets))]
-    for load in loads:
-        load.start()
-
+
+    loads[9].wait()
+    loads[10].wait()
     lane8 = lane_iota(8, 128)
     stacked = [jnp.concatenate([prior_ref[t], prior_ref[3 + t]], axis=0) for t in range(3)]
     for q in range(16):
@@ -234,6 +244,8 @@
     for edge in edges:
         edge.start()
 
+    loads[11].wait()
+    loads[12].wait()
     starts = []
     diagonal = lax.broadcasted_iota(jnp.int32, (COLS, COLS), 0) == lax.broadcasted_iota(jnp.int32, (COLS, COLS), 1)
     for p in range(2):
@@ -475,21 +487,21 @@
 
 def whole(prior, coil_maps, kspace, band_start, frac, mask):
     vmem = pl.BlockSpec(memory_space=pltpu.VMEM)
-    smem = pl.BlockSpec(memory_space=pltpu.SMEM)
-    far = pl.BlockSpec(memory_space=pl.ANY)
+    far = pl.BlockSpec(memory_space=pltpu.HBM)
     table = cosine_table()
     constants = (table, table.T) + place_tables() + return_tables()
     constants = [jnp.asarray(one, BF16) for one in constants]
-    moved = [kspace, frac] + constants
+    moved = [kspace, frac] + constants + [prior, coil_maps, band_start]
     return pl.pallas_call(
         whole_body,
         out_shape=(
             jax.ShapeDtypeStruct((COLS, LINES), F32),
             jax.ShapeDtypeStruct((ROWS, SLICES, READOUT), F32),
         ),
-        in_specs=[vmem, vmem, vmem, smem] + [far] * len(moved),
+        in_specs=[far] * (len(moved) + 1),
         out_specs=(vmem, vmem),
-        scratch_shapes=[pltpu.VMEM(one.shape, one.dtype) for one in moved]
+        scratch_shapes=[pltpu.SMEM(mask.shape, mask.dtype)]
+        + [pltpu.VMEM(one.shape, one.dtype) for one in moved]
         + [
             pltpu.VMEM((WIDE, 8, LINES), BF16),
             pltpu.VMEM((WIDE, 8, LINES), BF16),
@@ -504,7 +516,7 @@
             pltpu.VMEM((WIDE, 1, 128), F32),
             pltpu.VMEM((2, HALO, READOUT), BF16),
             pltpu.VMEM((2, HALO, READOUT), BF16),
-            pltpu.SemaphoreType.DMA((len(moved),)),
+            pltpu.SemaphoreType.DMA((len(moved) + 1,)),
             pltpu.SemaphoreType.DMA((2,)),
             pltpu.SemaphoreType.DMA((2,)),
             pltpu.SemaphoreType.DMA((2,)),
@@ -514,9 +526,9 @@
             pltpu.SemaphoreType.DMA((2,)),
             pltpu.SemaphoreType.DMA((2,)),
         ],
-        compiler_params=pltpu.CompilerParams(collective_id=0, has_side_effects=True, vmem_limit_bytes=48 << 20),
+        compiler_params=pltpu.CompilerParams(collective_id=0, has_side_effects=True, vmem_limit_bytes=63 << 20),
         name="whole",
-    )(prior, coil_maps, band_start, mask, *moved)
+    )(mask, *moved)
 
 
 def per_device(prior, coil_maps, kspace, band_start, band_frac, shot_mask):

time: 89.1 us -> 77.6 us (0.87)
  local copies, waits for them, and re-layouts: 13.1 us -> 2.01 us
    unnamed x28 -> x4, local copies, waits for them, and re-layouts: 13.1 us -> 2.01 us
where the time goes in v3:
time: 77.6 us; the launch traced here: 77.4 us
  Pallas kernels  74.8 us (96%)
  local copies, waits for them, and re-layouts  2.01 us (3%)
    pallas_call x1, Pallas kernels, whole(): pl.pallas_call(whole_body, out_shape=(jax.ShapeDtypeStruct((COLS, LINES),...  74.8 us
    unnamed x4, local copies, waits for them, and re-layouts  2.01 us

profile of v3, /device:TPU:1, one launch (start us, length us, event | category | flops | bytes accessed | tf_op | source)
XLA Modules:
  0.0 77.4 jit_solution(14461166663126725165)
XLA Ops:
  0.6 74.8 %whole.1 = (f32[24,384]{1,0:T(8,128)}, f32[6,4,384]{2,1,0:T(4,128)}) custom-call(s32[2,4,6]{2,1,0:T(4,128)} %bitcast.5, bf16[2,384,384]{2,1,0:T(8,128)(2,1)} %kspace_any.1, f32[2,24,384]{2,1,0:T(8,128)} %bitcast.3, bf16[384,384]{1,0:T(8,128)(2,1)} %constant.14.clone.table_any, bf16[384,384]{1,0:T(8,128)(2,1)} %constant.15.clone.turned_any, ...), custom_call_target="tpu_custom_call" | custom-call | tf_op jit(solution)/shard_map/whole/pallas_call | solution.py:495
  75.4 0.0 copy-start
  75.4 1.4 %copy.17 = f32[384,24]{0,1:T(8,128)} copy(f32[384,24]{0,1:T(8,128)} %bitcast.4) | data formatting | bytes 73728
  76.8 0.0 copy-done
  76.8 0.6 copy.18
Async XLA Ops:
  75.4 1.4 %copy-start = (f32[6,4,384]{2,1,0:T(4,128)S(1)}, f32[6,4,384]{2,1,0:T(4,128)}, u32[]{:S(2)}) copy-start(f32[6,4,384]{2,1,0:T(4,128)} %get-tuple-element.9) | copy-start | bytes 110596

commit v4 on v3

--- a/solution.py
+++ b/solution.py
@@ -15,6 +15,8 @@
 COILS = 16
 WIDE = 64
 NARROW = 8
+PLANE = 32
+LINE = 16
 LINES = 384
 COLS = 24
 ROWS = 6
@@ -170,7 +172,13 @@
     nme = lax.axis_index("narrow")
     my_slice = me // 16
     both = 2 * COLS
+    z_lo = me // 8
     barrier = pltpu.get_barrier_semaphore()
+
+    def far_first(k):
+        step = k // 8
+        half = lax.rem(z_lo // 4 + 1 - step // 4 + 2, 2)
+        return (4 * half + lax.rem(z_lo + 7 - step, 4)) * 8 + lax.rem(me + 7 - lax.rem(k, 8), 8)
 
     sources = (
         kspace_any, frac_any, table_any, turned_any, place_any, order_any, spread_any, rep_any, pick_any,
@@ -184,14 +192,38 @@
     for i in (9, 10, 11, 12, 1, 3, 0, 2, 4, 5, 6, 7, 8):
         loads[i].start()
 
-    @pl.loop(1, WIDE)
+    core, y_at = lax.rem(me, 2), lax.rem(me // 2, 4)
+    x_at, z_hi = lax.rem(nme, 4), nme // 4
+    z_at = z_hi * 8 + z_lo
+
+    def in_plane(a, b, c):
+        wide_to = z_lo * 8 + lax.rem(y_at + b, 4) * 2 + lax.rem(core + c, 2)
+        return {"wide": wide_to, "narrow": z_hi * 4 + lax.rem(x_at + a, 4)}
+
+    def in_line(a):
+        z_to = lax.rem(z_at + a, 16)
+        return {"wide": lax.rem(z_to, 8) * 8 + lax.rem(me, 8), "narrow": (z_to // 8) * 4 + x_at}
+
+    plane = [(a, b, c) for a in range(4) for b in range(4) for c in range(2) if (a, b, c) != (0, 0, 0)]
+    plane.sort(key=lambda at: -(min(at[0], 4 - at[0]) + min(at[1], 4 - at[1])))
+    line = sorted(range(1, 16), key=lambda a: -min(a, 16 - a))
+
+    @pl.loop(1, 8)
     def _(k):
-        pl.semaphore_signal(barrier, inc=1, device_id={"wide": lax.rem(me + k, WIDE)}, device_id_type=MESH)
+        other = {"wide": lax.rem(me + 8 * k, WIDE), "narrow": (1 - z_hi) * 4 + x_at}
+        pl.semaphore_signal(barrier, inc=1, device_id=other, device_id_type=MESH)
 
     @pl.loop(1, NARROW)
     def _(k):
         pl.semaphore_signal(barrier, inc=1, device_id={"narrow": lax.rem(nme + k, NARROW)}, device_id_type=MESH)
 
+    @pl.loop(0, WIDE - 1)
+    def _(k):
+        pl.semaphore_signal(barrier, inc=1, device_id={"wide": far_first(k)}, device_id_type=MESH)
+
+    for a, b, c in plane:
+        if a and (b or c):
+            pl.semaphore_signal(barrier, inc=1, device_id=in_plane(a, b, c), device_id_type=MESH)
 
     loads[9].wait()
     loads[10].wait()
@@ -213,10 +245,9 @@
             message = jnp.concatenate([block, packed[s : s + 1], packed[4 + s : 5 + s]], axis=0)
             send_maps[d] = message.astype(BF16)
 
-    pl.semaphore_wait(barrier, WIDE + NARROW - 2)
-
-    def to_wide(k, source, target, sems):
-        to = lax.rem(me + k, WIDE)
+    pl.semaphore_wait(barrier, WIDE + NARROW - 2 + 21 + 7)
+
+    def to_wide(to, source, target, sems):
         pltpu.make_async_remote_copy(
             src_ref=source(to), dst_ref=target, send_sem=sems.at[0], recv_sem=sems.at[1],
             device_id={"wide": to}, device_id_type=MESH,
@@ -229,7 +260,7 @@
 
     @pl.loop(1, WIDE)
     def _(k):
-        to_wide(k, lambda to: send_maps.at[to], got_ref.at[me], maps_sem)
+        to_wide(lax.rem(me + k, WIDE), lambda to: send_maps.at[to], got_ref.at[me], maps_sem)
 
     got_ref[me] = send_maps[me]
 
@@ -326,6 +357,31 @@
     back = through(residue)
     first = band_adjoint(jnp.concatenate([combine(back[p]) for p in range(2)], axis=0))
 
+    moved = band_apply(first)
+    squares = jnp.zeros((1, LINES), F32)
+    for p in range(2):
+        here = spectra(moved, p)
+        squares = squares + jnp.sum(here * here.astype(BF16).astype(F32), axis=0, keepdims=True)
+
+    def total(values):
+        return jnp.sum(jnp.sum(values, axis=0, keepdims=True), axis=1, keepdims=True)
+
+    lane1 = lane_iota(1, 128)
+    sums = jnp.zeros((1, 128), F32)
+    for i, part in enumerate((residue * residue, residue * first, first * first, squares)):
+        sums = jnp.where(lane1 == i, total(part), sums)
+    in_plane_at = x_at * 8 + lax.rem(me, 8)
+    near_sum[in_plane_at] = sums
+
+    def to_device(ref, slot, sems, device):
+        pltpu.make_async_remote_copy(
+            src_ref=ref.at[slot], dst_ref=ref.at[slot], send_sem=sems.at[0], recv_sem=sems.at[1],
+            device_id=device, device_id_type=MESH,
+        ).start()
+
+    for at in plane:
+        to_device(near_sum, in_plane_at, near_sem, in_plane(*at))
+
     fields = jnp.concatenate([residue, first, jnp.zeros((128 - 2 * COLS, LINES), F32)], axis=0)
     high = fields.astype(BF16)
     low = (fields - high.astype(F32)).astype(BF16)
@@ -344,34 +400,11 @@
                 packed = jnp.where((lane >= begin) & (lane < begin + 48), turned, packed)
         send_fields[:, row, :] = packed
 
-    @pl.loop(1, WIDE)
+    @pl.loop(0, WIDE - 1)
     def _(k):
-        to_wide(k, lambda to: send_fields.at[to], got_fields.at[me], field_sem)
+        to_wide(far_first(k), lambda to: send_fields.at[to], got_fields.at[me], field_sem)
 
     got_fields[me] = send_fields[me]
-
-    moved = band_apply(first)
-    squares = jnp.zeros((1, LINES), F32)
-    for p in range(2):
-        here = spectra(moved, p)
-        squares = squares + jnp.sum(here * here.astype(BF16).astype(F32), axis=0, keepdims=True)
-
-    def total(values):
-        return jnp.sum(jnp.sum(values, axis=0, keepdims=True), axis=1, keepdims=True)
-
-    lane1 = lane_iota(1, 128)
-    sums = jnp.zeros((1, 128), F32)
-    for i, part in enumerate((residue * residue, residue * first, first * first, squares)):
-        sums = jnp.where(lane1 == i, total(part), sums)
-    near_sum[nme] = sums
-
-    @pl.loop(1, NARROW)
-    def _(k):
-        to = lax.rem(nme + k, NARROW)
-        pltpu.make_async_remote_copy(
-            src_ref=near_sum.at[nme], dst_ref=near_sum.at[nme], send_sem=near_sem.at[0], recv_sem=near_sem.at[1],
-            device_id={"narrow": to}, device_id_type=MESH,
-        ).start()
 
     for edge in edges:
         edge.wait()
@@ -385,15 +418,12 @@
         rows += [jnp.zeros((16 - PLACES, READOUT), F32)]
         cells.append(jnp.concatenate(rows, axis=0))
 
-    finish(near_sum, near_sum, near_sem, NARROW - 1)
-    far_sum[me] = jnp.sum(near_sum[...].reshape(NARROW, 128), axis=0, keepdims=True)
-
-    @pl.loop(1, WIDE)
-    def _(k):
-        to_wide(k, lambda to: far_sum.at[me], far_sum.at[me], far_sem)
-
-    finish(far_sum, far_sum, far_sem, WIDE - 1)
-    sums = jnp.sum(far_sum[...].reshape(WIDE, 128), axis=0, keepdims=True)
+    finish(near_sum, near_sum, near_sem, PLANE - 1)
+    far_sum[z_at] = jnp.sum(near_sum[...].reshape(PLANE, 128), axis=0, keepdims=True)
+    for at in line:
+        to_device(far_sum, z_at, far_sem, in_line(at))
+    finish(far_sum, far_sum, far_sem, LINE - 1)
+    sums = jnp.sum(far_sum[...].reshape(LINE, 128), axis=0, keepdims=True)
     picked = [jnp.sum(jnp.where(lane1 == i, sums, 0.0), axis=1, keepdims=True) for i in range(4)]
     c0, c1 = step_scalars(*picked)
     solution_ref[...] = prior + c0 * residue + c1 * first
@@ -512,8 +542,8 @@
             pltpu.VMEM((2 * COLS, SPAN), jnp.int32),
             pltpu.VMEM((WIDE, DENSE, 128), F32),
             pltpu.VMEM((WIDE, DENSE, 128), F32),
-            pltpu.VMEM((NARROW, 1, 128), F32),
-            pltpu.VMEM((WIDE, 1, 128), F32),
+            pltpu.VMEM((PLANE, 1, 128), F32),
+            pltpu.VMEM((LINE, 1, 128), F32),
             pltpu.VMEM((2, HALO, READOUT), BF16),
             pltpu.VMEM((2, HALO, READOUT), BF16),
             pltpu.SemaphoreType.DMA((len(moved) + 1,)),

time: 77.6 us -> 69.1 us (0.89)
  Pallas kernels: 74.8 us -> 66.3 us
    pallas_call x1, Pallas kernels: 74.8 us -> 66.3 us  [whole(): pl.pallas_call(whole_body, out_shape=(jax.ShapeDtypeStruct((COLS, LINES),...]
where the time goes in v4:
time: 69.1 us; the launch traced here: 68.9 us
  Pallas kernels  66.3 us (96%)
  local copies, waits for them, and re-layouts  2.01 us (3%)
    pallas_call x1, Pallas kernels, whole(): pl.pallas_call(whole_body, out_shape=(jax.ShapeDtypeStruct((COLS, LINES),...  66.3 us
    unnamed x4, local copies, waits for them, and re-layouts  2.01 us

profile of v4, /device:TPU:1, one launch (start us, length us, event | category | flops | bytes accessed | tf_op | source)
XLA Modules:
  0.0 68.9 jit_solution(17269423739693962225)
XLA Ops:
  0.6 66.3 %whole.1 = (f32[24,384]{1,0:T(8,128)}, f32[6,4,384]{2,1,0:T(4,128)}) custom-call(s32[2,4,6]{2,1,0:T(4,128)} %bitcast.5, bf16[2,384,384]{2,1,0:T(8,128)(2,1)} %kspace_any.1, f32[2,24,384]{2,1,0:T(8,128)} %bitcast.3, bf16[384,384]{1,0:T(8,128)(2,1)} %constant.14.clone.table_any, bf16[384,384]{1,0:T(8,128)(2,1)} %constant.15.clone.turned_any, ...), custom_call_target="tpu_custom_call" | custom-call | tf_op jit(solution)/shard_map/whole/pallas_call | solution.py:525
  66.9 0.0 copy-start
  66.9 1.4 %copy.17 = f32[384,24]{0,1:T(8,128)} copy(f32[384,24]{0,1:T(8,128)} %bitcast.4) | data formatting | bytes 73728
  68.3 0.0 copy-done
  68.3 0.6 copy.18
Async XLA Ops:
  66.9 1.4 %copy-start = (f32[6,4,384]{2,1,0:T(4,128)S(1)}, f32[6,4,384]{2,1,0:T(4,128)}, u32[]{:S(2)}) copy-start(f32[6,4,384]{2,1,0:T(4,128)} %get-tuple-element.9) | copy-start | bytes 110596

commit v5 on v4

--- a/solution.py
+++ b/solution.py
@@ -26,6 +26,7 @@
 PIECES = 3
 EDGE = DIFF_STEPS
 PLACES = ROWS + 2 * EDGE
+PLACE_ROWS = (3, 4, 5, 6, 7, 8, 2, 9, 1, 10, 0, 11)
 DENSE = 5
 HALO = 24
 BAND_BITS = 5
@@ -67,7 +68,7 @@
     spread = np.zeros((PLACES * WIDE, LINES), np.float32)
     for i in range(PLACES):
         for w in range(WIDE):
-            line = ROWS * w - EDGE + i
+            line = ROWS * w - EDGE + PLACE_ROWS[i]
             if 0 <= line < LINES:
                 spread[i * WIDE + w, line] = 1.0
     rep = np.zeros((128, 2 * READOUT), np.float32)
@@ -78,7 +79,7 @@
     for i in range(2):
         for m in range(6):
             for w in range(WIDE):
-                pick[(w // 16) * 16 + 2 * m + i, (i * 6 + m) * WIDE + w] = 1.0
+                pick[(w // 16) * 16 + PLACE_ROWS[2 * m + i], (i * 6 + m) * WIDE + w] = 1.0
     return spread, rep, pick
 
 
@@ -165,14 +166,18 @@
     mask_ref, kspace_ref, frac_ref, table_ref, turned_ref, place_ref, order_ref, spread_ref, rep_ref, pick_ref,
     prior_ref, maps_ref, start_ref,
     send_maps, got_ref, edge_ref, maps3_ref, weight_ref, data_ref, start_rows_ref,
-    send_fields, got_fields, near_sum, far_sum, send_halo, got_halo,
+    send_fields, got_fields, near_sum, far_sum, send_halo, got_halo, got_cross, send_dia, got_dia,
     load_sem, maps_sem, edge_send, edge_recv, field_sem, near_sem, far_sem, halo_send, halo_recv,
+    cross_sem, near_cross, dia_sem,
 ):
     me = lax.axis_index("wide")
     nme = lax.axis_index("narrow")
     my_slice = me // 16
     both = 2 * COLS
     z_lo = me // 8
+    got_halo[...] = jnp.zeros(got_halo.shape, BF16)
+    got_cross[...] = jnp.zeros(got_cross.shape, F32)
+    got_dia[...] = jnp.zeros(got_dia.shape, F32)
     barrier = pltpu.get_barrier_semaphore()
 
     def far_first(k):
@@ -195,6 +200,10 @@
     core, y_at = lax.rem(me, 2), lax.rem(me // 2, 4)
     x_at, z_hi = lax.rem(nme, 4), nme // 4
     z_at = z_hi * 8 + z_lo
+    middle_pair = (nme == 3) | (nme == 4)
+    across_to = NARROW - 1 - nme
+    distance = jnp.where(nme == 3, SLICES - my_slice, my_slice + 1)
+    crosses = middle_pair & (distance <= EDGE)
 
     def in_plane(a, b, c):
         wide_to = z_lo * 8 + lax.rem(y_at + b, 4) * 2 + lax.rem(core + c, 2)
@@ -217,7 +226,7 @@
     def _(k):
         pl.semaphore_signal(barrier, inc=1, device_id={"narrow": lax.rem(nme + k, NARROW)}, device_id_type=MESH)
 
-    @pl.loop(0, WIDE - 1)
+    @pl.loop(0, WIDE - 1, unroll=9)
     def _(k):
         pl.semaphore_signal(barrier, inc=1, device_id={"wide": far_first(k)}, device_id_type=MESH)
 
@@ -258,7 +267,7 @@
         pltpu.make_async_copy(source.at[others], source.at[others], sems.at[0]).wait()
         pltpu.make_async_copy(target.at[others], target.at[others], sems.at[1]).wait()
 
-    @pl.loop(1, WIDE)
+    @pl.loop(1, WIDE, unroll=9)
     def _(k):
         to_wide(lax.rem(me + k, WIDE), lambda to: send_maps.at[to], got_ref.at[me], maps_sem)
 
@@ -400,7 +409,7 @@
                 packed = jnp.where((lane >= begin) & (lane < begin + 48), turned, packed)
         send_fields[:, row, :] = packed
 
-    @pl.loop(0, WIDE - 1)
+    @pl.loop(0, WIDE - 1, unroll=9)
     def _(k):
         to_wide(far_first(k), lambda to: send_fields.at[to], got_fields.at[me], field_sem)
 
@@ -418,10 +427,44 @@
         rows += [jnp.zeros((16 - PLACES, READOUT), F32)]
         cells.append(jnp.concatenate(rows, axis=0))
 
+    def diamond(near, middle, far):
+        return jnp.concatenate([near[1:11], middle[2:10], far[3:9]], axis=0)
+
+    send_dia[...] = jnp.where(nme == 3, diamond(cells[3], cells[2], cells[1]), diamond(cells[0], cells[1], cells[2]))
+    dia = pltpu.make_async_remote_copy(
+        src_ref=send_dia, dst_ref=got_dia, send_sem=dia_sem.at[0], recv_sem=dia_sem.at[1],
+        device_id={"narrow": across_to}, device_id_type=MESH,
+    )
+
+    @pl.when(middle_pair)
+    def _():
+        dia.start()
+
     finish(near_sum, near_sum, near_sem, PLANE - 1)
     far_sum[z_at] = jnp.sum(near_sum[...].reshape(PLANE, 128), axis=0, keepdims=True)
     for at in line:
         to_device(far_sum, z_at, far_sem, in_line(at))
+
+    def cross(rows, sems):
+        @pl.loop(0, WIDE, unroll=8)
+        def _(k):
+            step = k // 8
+            ahead_by = jnp.where(lax.rem(step, 2) == 1, (step + 1) // 2, 8 - step // 2)
+            to = lax.rem(z_lo + ahead_by, 8) * 8 + lax.rem(me + 4 + k, 8)
+            pltpu.make_async_remote_copy(
+                src_ref=send_fields.at[to, pl.ds(0, rows)], dst_ref=got_cross.at[me, pl.ds(0, rows)],
+                send_sem=sems.at[0], recv_sem=sems.at[1],
+                device_id={"wide": to, "narrow": across_to}, device_id_type=MESH,
+            ).start()
+
+    @pl.when(crosses & (distance == 1))
+    def _():
+        cross(4, near_cross)
+
+    @pl.when(crosses & (distance > 1))
+    def _():
+        cross(3, cross_sem)
+
     finish(far_sum, far_sum, far_sem, LINE - 1)
     sums = jnp.sum(far_sum[...].reshape(LINE, 128), axis=0, keepdims=True)
     picked = [jnp.sum(jnp.where(lane1 == i, sums, 0.0), axis=1, keepdims=True) for i in range(4)]
@@ -429,51 +472,88 @@
     solution_ref[...] = prior + c0 * residue + c1 * first
 
     finish(send_fields, got_fields, field_sem, WIDE - 1)
-    lines = [got_fields[:, row, :] for row in range(DENSE)]
-    pairs = []
-    for m in range(6):
-        begin = 96 * m
-        row, off = begin // 128, begin % 128
-        pair = pltpu.roll(lines[row], 128 - off, 1) if off else lines[row]
-        if off + 96 > 128:
-            pair = jnp.where(lane < 128 - off, pair, pltpu.roll(lines[row + 1], 128 - off, 1))
-        pairs.append(pair)
-    pairs = jnp.concatenate(pairs, axis=0)
-    joined = c0 * pairs + c1 * pltpu.roll(pairs, 128 - COLS, 1)
-    high = joined.astype(BF16)
-    low = (joined - high.astype(F32)).astype(BF16)
-    block_of = lax.broadcasted_iota(jnp.int32, (16, 2 * READOUT), 0)
-    readout_of = lax.rem(lane_iota(16, 2 * READOUT), READOUT)
-    inside = (readout_of >= COLS * block_of) & (readout_of < COLS * block_of + COLS)
-    change = jnp.zeros((SLICES * 16, READOUT), F32)
-    for part in (high, low):
-        wide = dot(part, rep_ref[...]).reshape(6 * SLICES, 16, 2 * READOUT)
-        wide = jnp.where(inside[None], wide, 0.0).reshape(6 * WIDE, 2 * READOUT).astype(BF16)
-        wide = jnp.concatenate([wide[:, :READOUT], wide[:, READOUT:]], axis=0)
-        change = change + dot(pick_ref[...], wide)
-    cells = [cells[s] + change[16 * s : 16 * s + 16] for s in range(SLICES)]
-
-    def diamond(near, middle, far):
-        rows = jnp.concatenate([near[1:11], middle[2:10], far[3:9]], axis=0)
-        return rows.astype(BF16)
-
-    send_halo[0] = diamond(cells[3], cells[2], cells[1])
-    send_halo[1] = diamond(cells[0], cells[1], cells[2])
-    halos = [
+    def unpack(source):
+        lines = [source[:, row, :] for row in range(DENSE)]
+        pairs = []
+        for m in range(6):
+            begin = 96 * m
+            row, off = begin // 128, begin % 128
+            pair = pltpu.roll(lines[row], 128 - off, 1) if off else lines[row]
+            if off + 96 > 128:
+                pair = jnp.where(lane < 128 - off, pair, pltpu.roll(lines[row + 1], 128 - off, 1))
+            pairs.append(pair)
+        pairs = jnp.concatenate(pairs, axis=0)
+        joined = c0 * pairs + c1 * pltpu.roll(pairs, 128 - COLS, 1)
+        high = joined.astype(BF16)
+        low = (joined - high.astype(F32)).astype(BF16)
+        block_of = lax.broadcasted_iota(jnp.int32, (16, 2 * READOUT), 0)
+        readout_of = lax.rem(lane_iota(16, 2 * READOUT), READOUT)
+        inside = (readout_of >= COLS * block_of) & (readout_of < COLS * block_of + COLS)
+        change = jnp.zeros((SLICES * 16, READOUT), F32)
+        for part in (high, low):
+            wide = dot(part, rep_ref[...]).reshape(6 * SLICES, 16, 2 * READOUT)
+            wide = jnp.where(inside[None], wide, 0.0).reshape(6 * WIDE, 2 * READOUT).astype(BF16)
+            wide = jnp.concatenate([wide[:, :READOUT], wide[:, READOUT:]], axis=0)
+            change = change + dot(pick_ref[...], wide)
+        return [change[16 * s : 16 * s + 16] for s in range(SLICES)]
+
+    change = unpack(got_fields)
+    cells = [cells[s] + change[s] for s in range(SLICES)]
+
+    send_halo[0] = diamond(cells[3], cells[2], cells[1]).astype(BF16)
+    send_halo[1] = diamond(cells[0], cells[1], cells[2]).astype(BF16)
+    up, down = (
         pltpu.make_async_remote_copy(
             src_ref=send_halo.at[side], dst_ref=got_halo.at[side],
             send_sem=halo_send.at[side], recv_sem=halo_recv.at[side],
             device_id={"narrow": lax.rem(nme + step, NARROW)}, device_id_type=MESH,
         )
         for side, step in ((0, 1), (1, NARROW - 1))
-    ]
-    for halo in halos:
-        halo.start()
-    for halo in halos:
-        halo.wait()
-
-    def opened(side, keep):
-        rows = got_halo[side].astype(F32) * keep
+    )
+
+    @pl.when(x_at < 3)
+    def _():
+        up.start()
+
+    @pl.when(x_at > 0)
+    def _():
+        down.start()
+
+    def wait_cross(ref, count, rows, sem):
+        part = ref.at[pl.ds(0, count), pl.ds(0, rows)]
+        pltpu.make_async_copy(part, part, sem).wait()
+
+    @pl.when(crosses & (distance == 1))
+    def _():
+        wait_cross(send_fields, WIDE, 4, near_cross.at[0])
+
+    @pl.when(crosses & (distance > 1))
+    def _():
+        wait_cross(send_fields, WIDE, 3, cross_sem.at[0])
+
+    @pl.when(middle_pair)
+    def _():
+        dia.wait()
+        wait_cross(got_cross, 16, 4, near_cross.at[1])
+        wait_cross(got_cross, 32, 3, cross_sem.at[1])
+
+    crossed = unpack(got_cross)
+    crossed = jnp.where(
+        nme == 3, diamond(crossed[0], crossed[1], crossed[2]), diamond(crossed[3], crossed[2], crossed[1])
+    )
+    crossed = crossed + got_dia[...]
+
+    @pl.when(x_at < 3)
+    def _():
+        up.wait_send()
+        down.wait_recv()
+
+    @pl.when(x_at > 0)
+    def _():
+        down.wait_send()
+        up.wait_recv()
+
+    def opened(rows):
         zero = jnp.zeros((8, READOUT), F32)
         near = jnp.concatenate([zero[:1], rows[:10], zero[:5]], axis=0)
         middle = jnp.concatenate([zero[:2], rows[10:18], zero[:6]], axis=0)
@@ -482,8 +562,8 @@
 
     has_low = jnp.where(nme > 0, 1.0, 0.0).astype(F32)
     has_high = jnp.where(nme < NARROW - 1, 1.0, 0.0).astype(F32)
-    near_low, mid_low, far_low = opened(0, has_low)
-    near_high, mid_high, far_high = opened(1, has_high)
+    near_low, mid_low, far_low = opened(jnp.where(nme == 4, crossed, got_halo[0].astype(F32)))
+    near_high, mid_high, far_high = opened(jnp.where(nme == 3, crossed, got_halo[1].astype(F32)))
     volume = [far_low, mid_low, near_low] + cells + [near_high, mid_high, far_high]
     keeps = [has_low] * 3 + [None] * SLICES + [has_high] * 3
     margin = jnp.zeros((16, 128), F32)
@@ -546,7 +626,13 @@
             pltpu.VMEM((LINE, 1, 128), F32),
             pltpu.VMEM((2, HALO, READOUT), BF16),
             pltpu.VMEM((2, HALO, READOUT), BF16),
+            pltpu.VMEM((WIDE, DENSE, 128), F32),
+            pltpu.VMEM((HALO, READOUT), F32),
+            pltpu.VMEM((HALO, READOUT), F32),
             pltpu.SemaphoreType.DMA((len(moved) + 1,)),
+            pltpu.SemaphoreType.DMA((2,)),
+            pltpu.SemaphoreType.DMA((2,)),
+            pltpu.SemaphoreType.DMA((2,)),
             pltpu.SemaphoreType.DMA((2,)),
             pltpu.SemaphoreType.DMA((2,)),
             pltpu.SemaphoreType.DMA((2,)),

time: 69.1 us -> 67.1 us (0.971); the launches traced: 68.9 us -> 66 us
  Pallas kernels: 66.3 us -> 63.3 us
    pallas_call x1, Pallas kernels: 66.3 us -> 63.3 us  [whole(): pl.pallas_call(whole_body, out_shape=(jax.ShapeDtypeStruct((COLS, LINES),...]
where the time goes in v5:
time: 67.1 us; the launch traced here: 66 us
  Pallas kernels  63.3 us (94%)
  local copies, waits for them, and re-layouts  2.01 us (3%)
    pallas_call x1, Pallas kernels, whole(): pl.pallas_call(whole_body, out_shape=(jax.ShapeDtypeStruct((COLS, LINES),...  63.3 us
    unnamed x4, local copies, waits for them, and re-layouts  2.01 us

profile of v5, /device:TPU:1, one launch (start us, length us, event | category | flops | bytes accessed | tf_op | source)
XLA Modules:
  0.0 66.0 jit_solution(9869092150515752241)
XLA Ops:
  0.6 63.3 %whole.1 = (f32[24,384]{1,0:T(8,128)}, f32[6,4,384]{2,1,0:T(4,128)}) custom-call(s32[2,4,6]{2,1,0:T(4,128)} %bitcast.5, bf16[2,384,384]{2,1,0:T(8,128)(2,1)} %kspace_any.1, f32[2,24,384]{2,1,0:T(8,128)} %bitcast.3, bf16[384,384]{1,0:T(8,128)(2,1)} %constant.14.clone.table_any, bf16[384,384]{1,0:T(8,128)(2,1)} %constant.15.clone.turned_any, ...), custom_call_target="tpu_custom_call" | custom-call | tf_op jit(solution)/shard_map/whole/pallas_call | solution.py:605
  63.9 0.0 copy-start
  63.9 1.4 %copy.17 = f32[384,24]{0,1:T(8,128)} copy(f32[384,24]{0,1:T(8,128)} %bitcast.4) | data formatting | bytes 73728
  65.3 0.0 copy-done
  65.3 0.6 copy.18
Async XLA Ops:
  63.9 1.4 %copy-start = (f32[6,4,384]{2,1,0:T(4,128)S(1)}, f32[6,4,384]{2,1,0:T(4,128)}, u32[]{:S(2)}) copy-start(f32[6,4,384]{2,1,0:T(4,128)} %get-tuple-element.9) | copy-start | bytes 110596

commit v6 on v5

--- a/solution.py
+++ b/solution.py
@@ -317,6 +317,31 @@
     for i in (2, 4, 5, 6, 7, 8):
         loads[i].wait()
 
+    for edge in edges:
+        edge.wait()
+    below = jnp.where(me > 0, 1.0, 0.0).astype(F32)
+    above = jnp.where(me < WIDE - 1, 1.0, 0.0).astype(F32)
+    cells = []
+    for s in range(SLICES):
+        rows = [edge_ref[0, i, s : s + 1, :] * below for i in range(EDGE)]
+        rows += [prior_ref[i, s : s + 1, :] for i in range(ROWS)]
+        rows += [edge_ref[1, i, s : s + 1, :] * above for i in range(EDGE)]
+        rows += [jnp.zeros((16 - PLACES, READOUT), F32)]
+        cells.append(jnp.concatenate(rows, axis=0))
+
+    def diamond(near, middle, far):
+        return jnp.concatenate([near[1:11], middle[2:10], far[3:9]], axis=0)
+
+    send_dia[...] = jnp.where(nme == 3, diamond(cells[3], cells[2], cells[1]), diamond(cells[0], cells[1], cells[2]))
+    dia = pltpu.make_async_remote_copy(
+        src_ref=send_dia, dst_ref=got_dia, send_sem=dia_sem.at[0], recv_sem=dia_sem.at[1],
+        device_id={"narrow": across_to}, device_id_type=MESH,
+    )
+
+    @pl.when(middle_pair)
+    def _():
+        dia.start()
+
     finish(send_maps, got_ref, maps_sem, WIDE - 1)
     got = got_ref[...].reshape(WIDE * 8, LINES)
     laid = dot_first(got, place_ref[...])
@@ -409,41 +434,18 @@
                 packed = jnp.where((lane >= begin) & (lane < begin + 48), turned, packed)
         send_fields[:, row, :] = packed
 
-    @pl.loop(0, WIDE - 1, unroll=9)
+    @pl.loop(0, WIDE // 2, unroll=8)
     def _(k):
         to_wide(far_first(k), lambda to: send_fields.at[to], got_fields.at[me], field_sem)
-
-    got_fields[me] = send_fields[me]
-
-    for edge in edges:
-        edge.wait()
-    below = jnp.where(me > 0, 1.0, 0.0).astype(F32)
-    above = jnp.where(me < WIDE - 1, 1.0, 0.0).astype(F32)
-    cells = []
-    for s in range(SLICES):
-        rows = [edge_ref[0, i, s : s + 1, :] * below for i in range(EDGE)]
-        rows += [prior_ref[i, s : s + 1, :] for i in range(ROWS)]
-        rows += [edge_ref[1, i, s : s + 1, :] * above for i in range(EDGE)]
-        rows += [jnp.zeros((16 - PLACES, READOUT), F32)]
-        cells.append(jnp.concatenate(rows, axis=0))
-
-    def diamond(near, middle, far):
-        return jnp.concatenate([near[1:11], middle[2:10], far[3:9]], axis=0)
-
-    send_dia[...] = jnp.where(nme == 3, diamond(cells[3], cells[2], cells[1]), diamond(cells[0], cells[1], cells[2]))
-    dia = pltpu.make_async_remote_copy(
-        src_ref=send_dia, dst_ref=got_dia, send_sem=dia_sem.at[0], recv_sem=dia_sem.at[1],
-        device_id={"narrow": across_to}, device_id_type=MESH,
-    )
-
-    @pl.when(middle_pair)
-    def _():
-        dia.start()
 
     finish(near_sum, near_sum, near_sem, PLANE - 1)
     far_sum[z_at] = jnp.sum(near_sum[...].reshape(PLANE, 128), axis=0, keepdims=True)
     for at in line:
         to_device(far_sum, z_at, far_sem, in_line(at))
+
+    @pl.loop(WIDE // 2, WIDE - 1)
+    def _(k):
+        to_wide(far_first(k), lambda to: send_fields.at[to], got_fields.at[me], field_sem)
 
     def cross(rows, sems):
         @pl.loop(0, WIDE, unroll=8)
@@ -464,6 +466,8 @@
     @pl.when(crosses & (distance > 1))
     def _():
         cross(3, cross_sem)
+
+    got_fields[me] = send_fields[me]
 
     finish(far_sum, far_sum, far_sem, LINE - 1)
     sums = jnp.sum(far_sum[...].reshape(LINE, 128), axis=0, keepdims=True)

time: 67.1 us -> 66.4 us (0.990)
  the two profiles are of different devices: /device:TPU:1 before, /device:TPU:385 now
where the time goes in v6:
time: 66.4 us; the launch traced here: 66.2 us
  Pallas kernels  63.6 us (96%)
  local copies, waits for them, and re-layouts  2.01 us (3%)
    pallas_call x1, Pallas kernels, whole(): pl.pallas_call(whole_body, out_shape=(jax.ShapeDtypeStruct((COLS, LINES),...  63.6 us
    unnamed x4, local copies, waits for them, and re-layouts  2.01 us

profile of v6, /device:TPU:385, one launch (start us, length us, event | category | flops | bytes accessed | tf_op | source)
XLA Modules:
  0.0 66.2 jit_solution(3398192132200986119)
XLA Ops:
  0.6 63.6 %whole.1 = (f32[24,384]{1,0:T(8,128)}, f32[6,4,384]{2,1,0:T(4,128)}) custom-call(s32[2,4,6]{2,1,0:T(4,128)} %bitcast.5, bf16[2,384,384]{2,1,0:T(8,128)(2,1)} %kspace_any.1, f32[2,24,384]{2,1,0:T(8,128)} %bitcast.3, bf16[384,384]{1,0:T(8,128)(2,1)} %constant.14.clone.table_any, bf16[384,384]{1,0:T(8,128)(2,1)} %constant.15.clone.turned_any, ...), custom_call_target="tpu_custom_call" | custom-call | tf_op jit(solution)/shard_map/whole/pallas_call | solution.py:609
  64.2 0.0 copy-start
  64.2 1.4 %copy.17 = f32[384,24]{0,1:T(8,128)} copy(f32[384,24]{0,1:T(8,128)} %bitcast.4) | data formatting | bytes 73728
  65.6 0.0 copy-done
  65.6 0.6 copy.18
Async XLA Ops:
  64.2 1.4 %copy-start = (f32[6,4,384]{2,1,0:T(4,128)S(1)}, f32[6,4,384]{2,1,0:T(4,128)}, u32[]{:S(2)}) copy-start(f32[6,4,384]{2,1,0:T(4,128)} %get-tuple-element.9) | copy-start | bytes 110596

commit v7 on v6

--- a/solution.py
+++ b/solution.py
@@ -194,7 +194,7 @@
         prior_ref, maps_ref, start_ref, mask_ref,
     )
     loads = [pltpu.make_async_copy(a, b, load_sem.at[i]) for i, (a, b) in enumerate(zip(sources, targets))]
-    for i in (9, 10, 11, 12, 1, 3, 0, 2, 4, 5, 6, 7, 8):
+    for i in (9, 10):
         loads[i].start()
 
     core, y_at = lax.rem(me, 2), lax.rem(me // 2, 4)
@@ -233,6 +233,9 @@
     for a, b, c in plane:
         if a and (b or c):
             pl.semaphore_signal(barrier, inc=1, device_id=in_plane(a, b, c), device_id_type=MESH)
+
+    for i in (11, 12, 1, 3, 0, 2, 4, 5, 6, 7, 8):
+        loads[i].start()
 
     loads[9].wait()
     loads[10].wait()

time: 66.4 us -> 66.4 us (level)
  the two profiles are of different devices: /device:TPU:385 before, /device:TPU:1 now
where the time goes in v7:
time: 66.4 us; the launch traced here: 65.2 us
  Pallas kernels  62.5 us (94%)
  local copies, waits for them, and re-layouts  2.01 us (3%)
    pallas_call x1, Pallas kernels, whole(): pl.pallas_call(whole_body, out_shape=(jax.ShapeDtypeStruct((COLS, LINES),...  62.5 us
    unnamed x4, local copies, waits for them, and re-layouts  2.01 us

profile of v7, /device:TPU:1, one launch (start us, length us, event | category | flops | bytes accessed | tf_op | source)
XLA Modules:
  0.0 65.2 jit_solution(6839541833246018679)
XLA Ops:
  0.6 62.5 %whole.1 = (f32[24,384]{1,0:T(8,128)}, f32[6,4,384]{2,1,0:T(4,128)}) custom-call(s32[2,4,6]{2,1,0:T(4,128)} %bitcast.5, bf16[2,384,384]{2,1,0:T(8,128)(2,1)} %kspace_any.1, f32[2,24,384]{2,1,0:T(8,128)} %bitcast.3, bf16[384,384]{1,0:T(8,128)(2,1)} %constant.14.clone.table_any, bf16[384,384]{1,0:T(8,128)(2,1)} %constant.15.clone.turned_any, ...), custom_call_target="tpu_custom_call" | custom-call | tf_op jit(solution)/shard_map/whole/pallas_call | solution.py:612
  63.1 0.0 copy-start
  63.1 1.4 %copy.17 = f32[384,24]{0,1:T(8,128)} copy(f32[384,24]{0,1:T(8,128)} %bitcast.4) | data formatting | bytes 73728
  64.5 0.0 copy-done
  64.5 0.6 copy.18
Async XLA Ops:
  63.1 1.4 %copy-start = (f32[6,4,384]{2,1,0:T(4,128)S(1)}, f32[6,4,384]{2,1,0:T(4,128)}, u32[]{:S(2)}) copy-start(f32[6,4,384]{2,1,0:T(4,128)} %get-tuple-element.9) | copy-start | bytes 110596
